TPU v7x, 32 devices: a whole 2x2x4 slice. The times are simulated.
32 devices in a mesh: gx: 8 (over z, y), gy: 4 (over x, core).
Axes of the slice: x: 2, y: 2, z: 4, core: 2. Of those that a mesh axis runs over, the one named last changes fastest.
Arguments:
- ocean_temp: float32 [64, 32, 1024], P(None, 'gy', 'gx'), may hold values from -2 to 1.5
- ocean_salt: float32 [64, 32, 1024], P(None, 'gy', 'gx'), may hold values from 33.8 to 34.8
- wet_mask: int32 [64, 32, 1024], P(None, 'gy', 'gx'), may hold values 0 or 1
- vertical_mix: float32 [32, 1024], P('gy', 'gx'), may hold values from 0.05 to 0.3
- friction: float32 [32, 1024], P('gy', 'gx'), may hold values from 0.5 to 5
- pressure: float32 [32, 1024], P('gy', 'gx'), may hold values from 200 to 1500
- pair_column: int32 [16384, 128], P(('gx', 'gy')), may hold values from 0 to 1023
- pair_weight: float32 [16384, 128], P(('gx', 'gy')), may hold values from 0.05 to 1
- block_owner: int32 [16384, 1], P(('gx', 'gy')), may hold values from 0 to 31; in each aligned block of 512 rows (0 to 511, 512 to 1023, ...) at most 32 rows name the same one
- block_target: int32 [16384], P(('gx', 'gy')), may hold values from 0 to 31
- enthalpy: float32 [40, 131072], P(None, ('gx', 'gy')), may hold values from -1 to 0.2
- surface_enthalpy: float32 [131072], P(('gx', 'gy')), may hold values from -1.5 to -0.5
- transition_layer: int32 [131072], P(('gx', 'gy')), may hold values from 0 to 40
- column_area: float32 [131072], P(('gx', 'gy')), may hold values from 0.5 to 2
Outputs:
- new_temp: float32 [64, 32, 1024], P(None, 'gy', 'gx')
- new_salt: float32 [64, 32, 1024], P(None, 'gy', 'gx')
- new_enthalpy: float32 [40, 131072], P(None, ('gx', 'gy'))
- ice_melt: float32 [131072], P(('gx', 'gy'))
Inputs may be any that keep to these rules, and one draw needn't show every extreme that they name: `block_owner`: of the 512 blocks of one device at most 32 name the same owner, and some owner gets exactly 32 of them.
All inputs are finite; a program needn't handle non-finite values. No bound on the sum of `wet_mask` on one device may be relied on, other than what follows from the above.
Results may differ from a plain program's by a relative error of at most 0.000059.
Values sent between devices are 32-bit elements; how exact they have to be, the bound alone decides.
A program may use at most 64 MiB of HBM per device.

v0:
```python
import jax
import jax.numpy as jnp
from jax import lax
from jax.sharding import PartitionSpec as P

mixing_rate = 0.2
liquidus_slope = -0.0573
liquidus_base = 0.0832
liquidus_depth = -0.000753
latent_ratio = 4.0
salt_ratio = 35.0
relax_rate = 0.1
cold_rate = 2.0
temperate_rate = 0.2


def padded(block, sides, width):
    for axis, dim in sides:
        count = lax.axis_size(axis)
        forward = [(i, i + 1) for i in range(count - 1)]
        backward = [(target, source) for source, target in forward]
        low = lax.ppermute(
            lax.slice_in_dim(block, block.shape[dim] - width, None, axis=dim), axis, forward
        )
        high = lax.ppermute(lax.slice_in_dim(block, 0, width, axis=dim), axis, backward)
        block = jnp.concatenate([low, block, high], axis=dim)
    return block


def spread_sideways(extended, wet_ext):
    middle = extended[:, :, 1:-1, 1:-1]
    wet_mid = wet_ext[:, 1:-1, 1:-1]
    height = middle.shape[2]
    breadth = middle.shape[3]
    change = jnp.zeros_like(middle)
    for row_off, col_off in ((0, 1), (2, 1), (1, 0), (1, 2)):
        beside = extended[:, :, row_off : row_off + height, col_off : col_off + breadth]
        wet_beside = wet_ext[:, row_off : row_off + height, col_off : col_off + breadth]
        change = change + (wet_mid * wet_beside)[None] * (beside - middle)
    return middle + mixing_rate * change


def mix_vertical(fields, wetness, vertical_mix):
    link = wetness[:-1] * wetness[1:]
    level_flux = vertical_mix[None, None] * link[None] * (fields[:, 1:] - fields[:, :-1])
    return (
        fields
        + jnp.pad(level_flux, ((0, 0), (0, 1), (0, 0), (0, 0)))
        - jnp.pad(level_flux, ((0, 0), (1, 0), (0, 0), (0, 0)))
    )


def shelf_melt(surface_temp, surface_salt, friction, pressure, wet_top):
    heat_gain = jnp.where(wet_top > 0, friction, 1.0)
    salt_safe = jnp.where(wet_top > 0, surface_salt, 34.0)
    salt_gain = heat_gain / salt_ratio
    curvature = heat_gain * liquidus_slope
    linear = (
        heat_gain * (surface_temp - liquidus_base - liquidus_depth * pressure)
        + latent_ratio * salt_gain
    )
    constant = latent_ratio * salt_gain * salt_safe
    boundary_salt = (
        2.0 * constant / (linear + jnp.sqrt(linear * linear - 4.0 * curvature * constant))
    )
    boundary_temp = liquidus_slope * boundary_salt + liquidus_base + liquidus_depth * pressure
    heat_flux = heat_gain * (surface_temp - boundary_temp) * wet_top
    salt_flux = salt_gain * (salt_safe - boundary_salt) * wet_top
    return (heat_flux, salt_flux, boundary_temp * wet_top)


def ocean_update(extended, wet_ext, vertical_mix, friction, pressure):
    fields = spread_sideways(extended, wet_ext)
    wetness = wet_ext[:, 1:-1, 1:-1]
    fields = mix_vertical(fields, wetness, vertical_mix)
    heat_flux, salt_flux, base_temp = shelf_melt(
        fields[0, 0], fields[1, 0], friction, pressure, wetness[0]
    )
    top_level = jnp.stack(
        [fields[0, 0] - relax_rate * heat_flux, fields[1, 0] - relax_rate * salt_flux]
    )
    fields = fields.at[:, 0].set(top_level)
    return (fields, heat_flux / latent_ratio, base_temp)


def solve_columns(enthalpy, transition_layer, surface_enthalpy, cover_sum, base_sum):
    layers = enthalpy.shape[0]
    level = jnp.arange(layers, dtype=jnp.int32)[:, None]
    rate = jnp.where(level < transition_layer[None, :], cold_rate, temperate_rate).astype(
        jnp.float32
    )
    inner = 0.5 * (rate[:-1] + rate[1:])
    zero_row = jnp.zeros_like(rate[:1])
    lower = jnp.concatenate([rate[:1], inner], axis=0)
    upper = jnp.concatenate([inner, cover_sum[None, :]], axis=0)
    diagonal = 1.0 + lower + upper
    below = -jnp.concatenate([zero_row, inner], axis=0)
    above = -jnp.concatenate([inner, zero_row], axis=0)
    right_side = enthalpy.at[0].add(rate[0] * surface_enthalpy).at[layers - 1].add(base_sum)

    def forward(carry, items):
        ratio_prev, value_prev = carry
        diag_now, below_now, above_now, side_now = items
        pivot = diag_now - below_now * ratio_prev
        ratio_now = above_now / pivot
        value_now = (side_now - below_now * value_prev) / pivot
        return ((ratio_now, value_now), (ratio_now, value_now))

    start = (jnp.zeros_like(rate[0]), jnp.zeros_like(rate[0]))
    unused, (ratios, values) = lax.scan(forward, start, (diagonal, below, above, right_side))

    def backward(next_value, items):
        ratio_now, value_now = items
        result = value_now - ratio_now * next_value
        return (result, result)

    unused_last, solved = lax.scan(
        backward, jnp.zeros_like(rate[0]), (ratios, values), reverse=True
    )
    return solved


def local(
    ocean_temp,
    ocean_salt,
    wet_mask,
    vertical_mix,
    friction,
    pressure,
    pair_column,
    pair_weight,
    block_owner,
    block_target,
    enthalpy,
    surface_enthalpy,
    transition_layer,
    column_area,
):
    levels = wet_mask.shape[0]
    wetness = wet_mask.astype(jnp.float32)
    fields = jnp.stack([ocean_temp, ocean_salt])
    statics = jnp.concatenate([wetness, jnp.stack([vertical_mix, friction, pressure])], axis=0)
    wide = padded(statics, (("gx", 2), ("gy", 1)), 2)
    wet_wide = wide[:levels]
    extended = padded(fields, (("gx", 3), ("gy", 2)), 2)
    first, melt_rate, base_temp = ocean_update(
        extended,
        wet_wide,
        wide[levels, 1:-1, 1:-1],
        wide[levels + 1, 1:-1, 1:-1],
        wide[levels + 2, 1:-1, 1:-1],
    )
    melt_total = melt_rate[1:-1, 1:-1]
    base_total = base_temp[1:-1, 1:-1]
    fields, melt_rate, base_temp = ocean_update(
        first, wet_wide[:, 1:-1, 1:-1], vertical_mix, friction, pressure
    )
    melt_total = melt_total + melt_rate
    base_total = base_total + base_temp
    mean_melt = (0.5 * melt_total).reshape(-1)
    mean_base = (0.5 * base_total).reshape(-1)
    count_x = lax.axis_size("gx")
    count_y = lax.axis_size("gy")
    devices = count_x * count_y
    blocks_here = pair_column.shape[0]
    block_width = pair_column.shape[1]
    capacity = max(2, (2 * blocks_here + devices - 1) // devices)
    owner = block_owner[:, 0]
    owner_hot = (owner[:, None] == jnp.arange(devices, dtype=jnp.int32)[None, :]).astype(jnp.int32)
    rank = jnp.sum(jnp.cumsum(owner_hot, axis=0) * owner_hot, axis=1) - 1
    slot = owner * capacity + rank
    payload = jnp.stack(
        [pair_weight * mean_melt[pair_column], pair_weight * mean_base[pair_column], pair_weight],
        axis=1,
    )
    send_values = jnp.zeros((devices * capacity, 3, block_width), jnp.float32).at[slot].set(payload)
    send_target = (
        jnp.full((devices * capacity,), -1.0, jnp.float32)
        .at[slot]
        .set(block_target.astype(jnp.float32))
    )
    got_values, got_target = (
        lax.all_to_all(
            send_values.reshape(devices, capacity, 3, block_width),
            ("gx", "gy"),
            split_axis=0,
            concat_axis=0,
            tiled=True,
        ),
        lax.all_to_all(
            send_target.reshape(devices, capacity),
            ("gx", "gy"),
            split_axis=0,
            concat_axis=0,
            tiled=True,
        ),
    )
    flat_values = got_values.reshape(devices * capacity, 3 * block_width)
    flat_target = got_target.reshape(devices * capacity)
    ice_cols = enthalpy.shape[1]
    ice_blocks = ice_cols // block_width
    target_hot = (
        flat_target[None, :] == jnp.arange(ice_blocks, dtype=jnp.int32).astype(jnp.float32)[:, None]
    ).astype(jnp.float32)
    gathered = jnp.dot(
        target_hot, flat_values, precision=lax.Precision.HIGHEST, preferred_element_type=jnp.float32
    )
    gathered = gathered.reshape(ice_blocks, 3, block_width)
    melt_sum = gathered[:, 0, :].reshape(ice_cols) / column_area
    base_sum = gathered[:, 1, :].reshape(ice_cols) / column_area
    cover_sum = gathered[:, 2, :].reshape(ice_cols) / column_area
    new_enthalpy = solve_columns(enthalpy, transition_layer, surface_enthalpy, cover_sum, base_sum)
    return (fields[0], fields[1], new_enthalpy, melt_sum)


def solution(mesh):
    return jax.shard_map(
        local,
        mesh=mesh,
        in_specs=(
            P(None, "gy", "gx"),
            P(None, "gy", "gx"),
            P(None, "gy", "gx"),
            P("gy", "gx"),
            P("gy", "gx"),
            P("gy", "gx"),
            P(("gx", "gy"), None),
            P(("gx", "gy"), None),
            P(("gx", "gy"), None),
            P(("gx", "gy")),
            P(None, ("gx", "gy")),
            P(("gx", "gy")),
            P(("gx", "gy")),
            P(("gx", "gy")),
        ),
        out_specs=(
            P(None, "gy", "gx"),
            P(None, "gy", "gx"),
            P(None, ("gx", "gy")),
            P(("gx", "gy")),
        ),
        check_vma=False,
    )
```

profile of v0, /device:TPU:0, one launch (start us, length us, event | category | flops | bytes accessed | tf_op | source)
XLA Modules:
  0.0 750.5 jit_solution(15057493863468311143)
XLA Ops:
  0.7 2.0 copy.69
  2.7 2.2 slice_maximum_fusion
  4.9 1.3 collective-permute-start.1
  6.2 5.5 collective-permute-start
  12.7 1.4 collective-permute-start.5
  14.1 5.4 collective-permute-start.4
  19.6 1.2 reduce-window.6
  21.2 2.4 scatter_custom_fusion
  24.3 6.3 all-to-all-start
  30.7 1.0 fusion.32
  31.8 13.5 %collective-permute-done.4 = f32[67,8,2]{2,1,0:T(8,128)S(1)} collective-permute-done((f32[67,8,2]{2,1,0:T(8,128)}, f32[67,8,2]{2,1,0:T(8,128)S(1)}, u32[]{:S(2)}, u32[]{:S(2)}) %collective-permute-start.4) | collective-permute-done | bytes 4320 | tf_op jit(solution)/shard_map/ppermute | solution.py:22
  45.8 1.9 collective-permute-start.6
  47.7 1.3 collective-permute-start.7
  50.3 1.3 collective-permute-start.3
  51.6 5.0 collective-permute-start.2
  58.5 1.2 slice_multiply_fusion.3
  60.2 1.0 pad_maximum_fusion.8
  61.2 4.0 fusion.8
  68.4 260.7 %gather_fusion = f32[65536]{0:T(1024)S(1)} fusion(f32[1024]{0:T(1024)S(1)} %get-tuple-element.282, s32[65536]{0:T(1024)S(1)} %fusion.32), kind=kCustom, calls=%fused_computation | custom fusion | bytes 786432 | tf_op jit(solution)/shard_map/gather | solution.py:173
  329.1 260.7 %gather_fusion.1 = f32[65536]{0:T(1024)S(1)} fusion(f32[1024]{0:T(1024)S(1)} %get-tuple-element.310, s32[65536]{0:T(1024)S(1)} %fusion.32), kind=kCustom, calls=%fused_computation.1 | custom fusion | bytes 786432 | tf_op jit(solution)/shard_map/gather | solution.py:173
  590.8 13.6 %scatter_fusion = f32[1024,3,128]{2,1,0:T(4,128)S(1)} fusion(f32[1024,3,128]{2,1,0:T(4,128)S(1)} %broadcast_in_dim.80, s32[512]{0:T(512)S(1)} %bitcast.269, f32[512,3,128]{2,1,0:T(4,128)S(1)} %copy.24), kind=kCustom, calls=%fused_computation.3 | custom fusion | bytes 2361344 | tf_op jit(solution)/shard_map/scatter | solution.py:176
  604.4 1.4 copy.26
  605.8 8.0 %all-to-all-start.1 = ((f32[32,32,3,128]{3,1,2,0:T(8,128)}), f32[32,32,3,128]{3,1,2,0:T(8,128)S(1)}, u32[]{:S(2)}, u32[]{:S(2)}) async-start(f32[32,32,3,128]{3,1,2,0:T(8,128)} %copy.26), calls=%async_computation.1 | async-start | bytes 3145728 | tf_op jit(solution)/shard_map/all_to_all | solution.py:183
  613.9 1.0 slice_add_fusion.2
  614.9 1.6 scatter-add.6
  618.0 1.4 reduce.13
  620.3 31.1 %all-to-all-done.1 = f32[32,32,3,128]{3,1,2,0:T(8,128)S(1)} async-done(((f32[32,32,3,128]{3,1,2,0:T(8,128)}), f32[32,32,3,128]{3,1,2,0:T(8,128)S(1)}, u32[]{:S(2)}, u32[]{:S(2)}) %all-to-all-start.1) | async-done | bytes 1572896 | tf_op jit(solution)/shard_map/all_to_all | solution.py:183
  651.3 1.3 copy.27
  656.0 1.6 scatter-add.9
  657.8 72.8 %while.38 = (s32[]{:T(128)}, f32[4096]{0:T(1024)S(1)}, f32[4096]{0:T(1024)S(1)}, f32[40,4096]{1,0:T(8,128)S(1)}, f32[40,4096]{1,0:T(8,128)S(1)}, /*index=5*/f32[...) while((s32[]{:T(128)}, f32[4096]{0:T(1024)S(1)}, ...), condition=%wide.region_6.7_spmd.clone, body=%wide.region_5.6_spmd.clone.sunk | while | flops 32771 | bytes 327823 | solution.py:110
  665.1 0.9 constant_dynamic-slice_fusion.9
  730.6 19.0 %while.39 = (s32[]{:T(128)}, f32[4096]{0:T(1024)S(1)}, f32[40,4096]{1,0:T(8,128)S(1)}, f32[40,4096]{1,0:T(8,128)S(1)}, f32[40,4096]{1,0:T(8,128)S(1)}, /*index=5*/s32[]{:T(128)}, s32[]{:T(128)}, s32[]{:T(128)}) while((s32[]{:T(128)}, f32[4096]{0:T(1024)S(1)}, f32[40,4096]{1,0:T(8,128)S(1)}, f32[40,4096]{1,0:T(8,128)S(1)}, ...), condition=%wide.region_8.9_spmd.clone, body=%wide.region_7.8_spmd.clone.sunk | while | flops 12292 | bytes 163963 | solution.py:117
  (431 shorter events, 104.0 us)
Async XLA Ops:
  0.6 11.1 %copy-start.12 = (s32[64,8,128]{2,1,0:T(8,128)S(1)}, s32[64,8,128]{2,1,0:T(8,128)}, u32[]{:S(2)}) copy-start(s32[64,8,128]{2,1,0:T(8,128)} %param.28) | copy-start | bytes 786436
  0.6 11.1 %copy-start.13 = (f32[8,128]{1,0:T(8,128)S(1)}, f32[8,128]{1,0:T(8,128)}, u32[]{:S(2)}) copy-start(f32[8,128]{1,0:T(8,128)} %param.29) | copy-start | bytes 12292
  0.7 11.1 %copy-start.11 = (f32[8,128]{1,0:T(8,128)S(1)}, f32[8,128]{1,0:T(8,128)}, u32[]{:S(2)}) copy-start(f32[8,128]{1,0:T(8,128)} %param.30) | copy-start | bytes 12292
  0.7 11.1 %copy-start.10 = (f32[8,128]{1,0:T(8,128)S(1)}, f32[8,128]{1,0:T(8,128)}, u32[]{:S(2)}) copy-start(f32[8,128]{1,0:T(8,128)} %param.31) | copy-start | bytes 12292
  2.7 16.9 %copy-start.14 = (s32[512,1]{0,1:T(1,128)S(1)}, s32[512,1]{0,1:T(1,128)}, u32[]{:S(2)}) copy-start(s32[512,1]{0,1:T(1,128)} %param.34) | copy-start | bytes 6148
  2.7 18.5 %copy-start.22 = (s32[512]{0:T(512)S(1)}, s32[512]{0:T(512)}, u32[]{:S(2)}) copy-start(s32[512]{0:T(512)} %param.35) | copy-start | bytes 6148
  4.9 44.5 %collective-permute-start.1 = (f32[2,64,8,2]{3,2,1,0:T(8,128)}, f32[2,64,8,2]{3,2,1,0:T(8,128)S(1)}, u32[]{:S(2)}, u32[]{:S(2)}) collective-permute-start(f32[2,64,8,2]{3,2,1,0:T(8,128)} %get-tuple-element.319), channel_id=1, source_target_pairs={{4,0},{8,4},{12,8},{16,12},{20,16},{24,20},{28,24},{5,1},{9,5},{13... | collective-permute-start | bytes 24584 | tf_op jit(solution)/shard_map/ppermute | solution.py:25
  6.2 43.2 %collective-permute-start = (f32[2,64,8,2]{3,2,1,0:T(8,128)S(1)}, f32[2,64,8,2]{3,2,1,0:T(8,128)S(1)}, u32[]{:S(2)}, u32[]{:S(2)}) collective-permute-start(f32[2,64,8,2]{3,2,1,0:T(8,128)S(1)} %get-tuple-element.318), channel_id=1, source_target_pairs={{0,4},{4,8},{8,12},{12,16},{16,20},{20,24},{24,28},{1,5},{5,9},{9,... | collective-permute-start | bytes 24584 | tf_op jit(solution)/shard_map/ppermute | solution.py:22
  12.7 36.7 %copy-start = (f32[64,8,128]{2,1,0:T(8,128)S(1)}, f32[64,8,128]{2,1,0:T(8,128)}, u32[]{:S(2)}) copy-start(f32[64,8,128]{2,1,0:T(8,128)} %param.27) | copy-start | bytes 786436
  12.7 36.7 %copy-start.1 = (f32[64,8,128]{2,1,0:T(8,128)S(1)}, f32[64,8,128]{2,1,0:T(8,128)}, u32[]{:S(2)}) copy-start(f32[64,8,128]{2,1,0:T(8,128)} %param.26) | copy-start | bytes 786436
  12.7 19.1 %collective-permute-start.5 = (f32[67,8,2]{2,1,0:T(8,128)}, f32[67,8,2]{2,1,0:T(8,128)S(1)}, u32[]{:S(2)}, u32[]{:S(2)}) collective-permute-start(f32[67,8,2]{2,1,0:T(8,128)} %get-tuple-element.323), channel_id=1, source_target_pairs={{4,0},{8,4},{12,8},{16,12},{20,16},{24,20},{28,24},{5,1},{9,5},{13... | collective-permute-start | bytes 12872 | tf_op jit(solution)/shard_map/ppermute | solution.py:25
  14.1 31.2 %collective-permute-start.4 = (f32[67,8,2]{2,1,0:T(8,128)}, f32[67,8,2]{2,1,0:T(8,128)S(1)}, u32[]{:S(2)}, u32[]{:S(2)}) collective-permute-start(f32[67,8,2]{2,1,0:T(8,128)} %get-tuple-element.322), channel_id=1, source_target_pairs={{0,4},{4,8},{8,12},{12,16},{16,20},{20,24},{24,28},{1,5},{5,9},{9,... | collective-permute-start | bytes 12872 | tf_op jit(solution)/shard_map/ppermute | solution.py:22
  21.2 9.5 %copy-start.20 = (s32[512,1]{0,1:T(1,128)}, s32[512,1]{0,1:T(1,128)S(1)}, u32[]{:S(2)}) copy-start(s32[512,1]{0,1:T(1,128)S(1)} %compare_select_fusion.2) | copy-start | bytes 6148
  24.3 581.4 %all-to-all-start = ((f32[32,1,32]{2,1,0:T(1,128)}), f32[32,1,32]{2,1,0:T(1,128)}, u32[]{:S(2)}, u32[]{:S(2)}) async-start(f32[32,1,32]{2,1,0:T(1,128)} %all_to_all.9), calls=%async_computation | async-start | bytes 32768 | tf_op jit(solution)/shard_map/all_to_all | solution.py:190
  45.8 10.8 %collective-permute-start.6 = (f32[67,2,132]{2,1,0:T(2,128)S(1)}, f32[67,2,132]{2,1,0:T(2,128)S(1)}, u32[]{:S(2)}, u32[]{:S(2)}) collective-permute-start(f32[67,2,132]{2,1,0:T(2,128)S(1)} %get-tuple-element.308), channel_id=1, source_target_pairs={{0,1},{1,2},{2,3},{4,5},{5,6},{6,7},{8,9},{9,10},{10,11},{12,13},{... | collective-permute-start | bytes 212264 | tf_op jit(solution)/shard_map/ppermute | solution.py:22
  47.7 8.8 %collective-permute-start.7 = (f32[67,2,132]{2,1,0:T(2,128)S(1)}, f32[67,2,132]{2,1,0:T(2,128)S(1)}, u32[]{:S(2)}, u32[]{:S(2)}) collective-permute-start(f32[67,2,132]{2,1,0:T(2,128)S(1)} %get-tuple-element.309), channel_id=1, source_target_pairs={{1,0},{2,1},{3,2},{5,4},{6,5},{7,6},{9,8},{10,9},{11,10},{13,12},{... | collective-permute-start | bytes 212264 | tf_op jit(solution)/shard_map/ppermute | solution.py:25
  50.3 9.9 %collective-permute-start.3 = (f32[2,64,2,132]{3,2,1,0:T(2,128)S(1)}, f32[2,64,2,132]{3,2,1,0:T(2,128)S(1)}, u32[]{:S(2)}, u32[]{:S(2)}) collective-permute-start(f32[2,64,2,132]{3,2,1,0:T(2,128)S(1)} %get-tuple-element.298), channel_id=1, source_target_pairs={{1,0},{2,1},{3,2},{5,4},{6,5},{7,6},{9,8},{10,9},{11,10},{13,12},{... | collective-permute-start | bytes 405512 | tf_op jit(solution)/shard_map/ppermute | solution.py:25
  51.6 8.6 %collective-permute-start.2 = (f32[2,64,2,132]{3,2,1,0:T(2,128)S(1)}, f32[2,64,2,132]{3,2,1,0:T(2,128)S(1)}, u32[]{:S(2)}, u32[]{:S(2)}) collective-permute-start(f32[2,64,2,132]{3,2,1,0:T(2,128)S(1)} %get-tuple-element.297), channel_id=1, source_target_pairs={{0,1},{1,2},{2,3},{4,5},{5,6},{6,7},{8,9},{9,10},{10,11},{12,13},{... | collective-permute-start | bytes 405512 | tf_op jit(solution)/shard_map/ppermute | solution.py:22
  67.7 261.4 %copy-start.3 = (f32[2,64,8,128]{3,2,1,0:T(8,128)}, f32[2,64,8,128]{3,2,1,0:T(8,128)S(1)}, u32[]{:S(2)}) copy-start(f32[2,64,8,128]{3,2,1,0:T(8,128)S(1)} %pad_subtract_fusion.1) | copy-start | bytes 1572868
  329.1 260.7 %copy-start.8 = (f32[512,128]{1,0:T(8,128)S(1)}, f32[512,128]{1,0:T(8,128)}, u32[]{:S(2)}) copy-start(f32[512,128]{1,0:T(8,128)} %param.33) | copy-start | bytes 786436
  589.9 0.8 copy-start.21
  605.8 8.0 %copy-start.19 = (s32[4096]{0:T(1024)S(1)}, s32[4096]{0:T(1024)}, u32[]{:S(2)}) copy-start(s32[4096]{0:T(1024)} %param.38) | copy-start | bytes 49156
  605.8 8.2 %copy-start.15 = (f32[4096]{0:T(1024)S(1)}, f32[4096]{0:T(1024)}, u32[]{:S(2)}) copy-start(f32[4096]{0:T(1024)} %param.37) | copy-start | bytes 49156
  605.8 45.6 %all-to-all-start.1 = ((f32[32,32,3,128]{3,1,2,0:T(8,128)}), f32[32,32,3,128]{3,1,2,0:T(8,128)S(1)}, u32[]{:S(2)}, u32[]{:S(2)}) async-start(f32[32,32,3,128]{3,1,2,0:T(8,128)} %copy.26), calls=%async_computation.1 | async-start | bytes 3145728 | tf_op jit(solution)/shard_map/all_to_all | solution.py:183
  613.8 5.6 copy-start.4
  613.8 5.6 copy-start.17
  613.8 5.6 copy-start.18
  652.8 1.4 copy-start.16
  653.3 1.6 copy-start.2
  654.2 3.6 copy-start.6
  654.2 3.6 copy-start.7
  655.1 75.5 %copy-start.5 = (f32[4096]{0:T(1024)S(1)}, f32[4096]{0:T(1024)}, u32[]{:S(2)}) copy-start(f32[4096]{0:T(1024)} %custom-call.2) | copy-start | bytes 49156
  (1 other events, 0.8 us)
where the time goes:
time: 752 us; the launch traced here: 750 us
  local copies, waits for them, and re-layouts  638 us (85%)
  waiting for transfers between devices  44.6 us (6%)
  starting transfers between devices  37.5 us (5%)
  other arithmetic  24.2 us (3%)
    gather x1, local copies, waits for them, and re-layouts, local(): mean_base[pair_column]  261 us
    gather x1, local copies, waits for them, and re-layouts, local(): mean_melt[pair_column]  261 us
    dynamic_update_slice x120, local copies, waits for them, and re-layouts, solve_columns(): lax.scan(forward, start, (diagonal, below, above, right_side))  47.2 us
    dynamic_slice x120, local copies, waits for them, and re-layouts, solve_columns(): lax.scan(forward, start, (diagonal, below, above, right_side))  39.9 us
    all_to_all x1, waiting for transfers between devices, local(): lax.all_to_all(send_values.reshape(devices, capacity, 3, block_width), ('...  31.1 us
    ppermute x4, starting transfers between devices, padded(): lax.ppermute(lax.slice_in_dim(block, block.shape[dim] - width, None, axis...  17.8 us
  transfers between devices with their start and end apart: 10, of which 2 were waited for; matrix products, arithmetic and copies ran while one was open for 75% of the time, Pallas kernels for 0%

commit v1 on v0

v1 whole, which is shorter than its diff:
```python
import functools

import jax
import jax.numpy as jnp
from jax import lax
from jax.experimental import pallas as pl
from jax.experimental.pallas import tpu as pltpu
from jax.sharding import PartitionSpec as P

mixing_rate = 0.2
liquidus_slope = -0.0573
liquidus_base = 0.0832
liquidus_depth = -0.000753
latent_ratio = 4.0
salt_ratio = 35.0
relax_rate = 0.1
cold_rate = 2.0
temperate_rate = 0.2

MESH = pl.DeviceIdType.MESH
CHUNK = 8


def shelf_melt(surface_temp, surface_salt, friction, pressure, wet_top):
    heat_gain = jnp.where(wet_top > 0, friction, 1.0)
    salt_safe = jnp.where(wet_top > 0, surface_salt, 34.0)
    salt_gain = heat_gain / salt_ratio
    curvature = heat_gain * liquidus_slope
    linear = (
        heat_gain * (surface_temp - liquidus_base - liquidus_depth * pressure)
        + latent_ratio * salt_gain
    )
    constant = latent_ratio * salt_gain * salt_safe
    boundary_salt = (
        2.0 * constant / (linear + jnp.sqrt(linear * linear - 4.0 * curvature * constant))
    )
    boundary_temp = liquidus_slope * boundary_salt + liquidus_base + liquidus_depth * pressure
    heat_flux = heat_gain * (surface_temp - boundary_temp) * wet_top
    salt_flux = salt_gain * (salt_safe - boundary_salt) * wet_top
    return (heat_flux, salt_flux, boundary_temp * wet_top)


def digits(axis, size):
    found = []
    base = 1
    while size > 1:
        radix = next(p for p in range(2, size + 1) if size % p == 0)
        found.append((axis, base, radix))
        base *= radix
        size //= radix
    return found


def stage_orders(nx, ny):
    gy = digits("gy", ny)
    gx = digits("gx", nx)
    first = gy + gx
    second = gy[:1] + gx[:1] + gy[1:] + gx[1:]
    return (first, second)


def slot_of(owner, order, ny):
    coord = {"gx": owner // ny, "gy": owner % ny}
    place = jnp.zeros_like(owner)
    for axis, base, radix in order:
        place = place * radix + (coord[axis] // base) % radix
    return place


def live_rows(order, total):
    rows = [total]
    for _, _, radix in order:
        rows.append(rows[-1] // radix)
    return rows


def split_two(value):
    high = value.astype(jnp.bfloat16)
    low = (value - high.astype(jnp.float32)).astype(jnp.bfloat16)
    return high, low


def kernel(sizes, orders, *refs):
    nx, ny, levels, cj, ci, targets, layers = sizes
    refs = list(refs)

    def take(count):
        out = refs[:count]
        del refs[:count]
        return out

    (temp, salt, wet, vmix, fric, pres, pcol, pw, seg_a, seg_b, enth, surf, trans, area) = take(14)
    (out_temp, out_salt, out_enth, out_melt) = take(4)
    (wetp, coef, mid, edge, first) = take(5)
    (row_send, row_recv, col_send, col_recv) = take(4)
    (row_send2, row_recv2, col_send2, col_recv2) = take(4)
    (hot, pay, ratios, values) = take(4)
    chains = []
    for order in (orders[0], orders[1], orders[0]):
        live = take(len(order) + 1)
        got = take(len(order))
        send_sem, recv_sem = take(2)
        chains.append((order, live, got, send_sem, recv_sem))
    (halo_send, halo_recv) = take(2)

    gx = lax.axis_index("gx")
    gy = lax.axis_index("gy")
    coord = {"gx": gx, "gy": gy}
    span = cj * CHUNK
    chunks = levels // CHUNK
    cells = levels * cj
    blocks = pcol.shape[0]
    width = pcol.shape[1]

    sides = (
        (gy > 0, {"gy": gy - 1}),
        (gy < ny - 1, {"gy": gy + 1}),
        (gx > 0, {"gx": gx - 1}),
        (gx < nx - 1, {"gx": gx + 1}),
    )

    for buf in (row_recv, row_recv2):
        for side in range(2):
            @pl.when(jnp.logical_not(sides[side][0]))
            def _():
                buf[side] = jnp.zeros(buf.shape[1:], jnp.float32)
    for buf in (col_recv, col_recv2):
        for side in range(2):
            @pl.when(jnp.logical_not(sides[2 + side][0]))
            def _():
                buf[side] = jnp.zeros(buf.shape[1:], jnp.float32)

    barrier = pltpu.get_barrier_semaphore()
    partners = 0
    for there, device in sides:
        @pl.when(there)
        def _():
            pl.semaphore_signal(barrier, inc=1, device_id=device, device_id_type=MESH)
        partners = partners + there.astype(jnp.int32)
    for axis, base, radix in orders[0]:
        mine = (coord[axis] // base) % radix
        for j in range(1, radix):
            peer = {axis: coord[axis] + ((mine + j) % radix - mine) * base}
            pl.semaphore_signal(barrier, inc=1, device_id=peer, device_id_type=MESH)
            partners = partners + 1

    zeros_pad = jnp.zeros((cj, ci), jnp.float32)
    wetp[pl.ds(0, cj), :] = zeros_pad
    wetp[pl.ds(cj + cells, cj), :] = zeros_pad
    wetp[pl.ds(cj, cells), :] = wet[...].astype(jnp.float32)
    for q in range(2):
        mid[q, pl.ds(0, cj), :] = zeros_pad
        mid[q, pl.ds(cj + cells, cj), :] = zeros_pad

    def pack(q, source, offset, rows, cols):
        rows[0, q] = source[pl.ds(offset, levels, stride=cj), :]
        rows[1, q] = source[pl.ds(offset + cj - 1, levels, stride=cj), :]
        turned = source[pl.ds(offset, cells), :].T
        cols[0, pl.ds(q, 1), :] = turned[0:1]
        cols[1, pl.ds(q, 1), :] = turned[ci - 1 : ci]

    for cols in (col_send, col_send2):
        cols[...] = jnp.zeros(cols.shape, jnp.float32)
    pack(0, temp, 0, row_send, col_send)
    pack(1, salt, 0, row_send, col_send)
    pack(2, wetp, cj, row_send, col_send)

    pl.semaphore_wait(barrier, partners)

    def halo(step, rows, rows_in, cols, cols_in):
        copies = []
        for side, (there, device) in enumerate(sides):
            src, dst = (rows, rows_in) if side < 2 else (cols, cols_in)
            copies.append(
                pltpu.make_async_remote_copy(
                    src_ref=src.at[side % 2],
                    dst_ref=dst.at[1 - side % 2],
                    send_sem=halo_send.at[step, side],
                    recv_sem=halo_recv.at[step, side - side % 2 + 1 - side % 2],
                    device_id=device,
                    device_id_type=MESH,
                )
            )
        return copies

    def halo_start(copies):
        for (there, _), copy in zip(sides, copies):
            @pl.when(there)
            def _():
                copy.start()

    def halo_wait(copies):
        for side, (there, _) in enumerate(sides):
            opposite = copies[side - side % 2 + 1 - side % 2]

            @pl.when(there)
            def _():
                opposite.wait_recv()

    def halo_done(copies):
        for (there, _), copy in zip(sides, copies):
            @pl.when(there)
            def _():
                copy.wait_send()

    halo1 = halo(0, row_send, row_recv, col_send, col_recv)
    halo_start(halo1)

    def make_copies(chain, stage):
        order, live, got, send_sem, recv_sem = chain
        axis, base, radix = order[stage]
        rows = live[stage + 1].shape[0]
        mine = (coord[axis] // base) % radix
        copies = []
        for j in range(1, radix):
            digit = (mine + j) % radix
            copies.append(
                pltpu.make_async_remote_copy(
                    src_ref=live[stage].at[pl.ds(digit * rows, rows)],
                    dst_ref=got[stage].at[j - 1],
                    send_sem=send_sem.at[stage, j - 1],
                    recv_sem=recv_sem.at[stage, j - 1],
                    device_id={axis: coord[axis] + (digit - mine) * base},
                    device_id_type=MESH,
                )
            )
        return copies

    def start_stage(chain, stage):
        for copy in make_copies(chain, stage):
            copy.start()

    def end_stage(chain, stage):
        order, live, got, _, _ = chain
        axis, base, radix = order[stage]
        rows = live[stage + 1].shape[0]
        mine = (coord[axis] // base) % radix
        total = live[stage][pl.ds(pl.multiple_of(mine * rows, rows), rows), :]
        for copy in make_copies(chain, stage):
            copy.wait_recv()
        for j in range(1, radix):
            total = total + got[stage][j - 1]
        live[stage + 1][...] = total
        if stage + 1 < len(order):
            start_stage(chain, stage + 1)

    def drain(chain):
        for stage in range(len(chain[0])):
            for copy in make_copies(chain, stage):
                copy.wait_send()

    seg_total = chains[0][1][0].shape[0]
    hot_rows = 256

    def build_hot(which, seg):
        def body(i, carry):
            start = pl.multiple_of(i * hot_rows, hot_rows)
            row = lax.broadcasted_iota(jnp.int32, (hot_rows, blocks), 0) + start
            hit = (row == seg[...]).astype(jnp.float32)
            hot[which, pl.ds(start, hot_rows), :] = hit.astype(jnp.bfloat16)
            return carry

        lax.fori_loop(0, seg_total // hot_rows, body, 0)

    def sum_blocks(which, slot, target):
        def body(i, carry):
            start = pl.multiple_of(i * hot_rows, hot_rows)
            both = jnp.dot(
                hot[which, pl.ds(start, hot_rows), :],
                pay[slot],
                preferred_element_type=jnp.float32,
            )
            target[pl.ds(start, hot_rows), :] = both[:, :width] + both[:, width:]
            return carry

        lax.fori_loop(0, seg_total // hot_rows, body, 0)

    build_hot(0, seg_a)
    high, low = split_two(pw[...])
    pay[2, :, pl.ds(0, width)] = high
    pay[2, :, pl.ds(width, width)] = low
    sum_blocks(0, 2, chains[2][1][0])
    start_stage(chains[2], 0)
    build_hot(1, seg_b)

    lane = lax.broadcasted_iota(jnp.int32, (CHUNK, cj, ci), 2)
    row = lax.broadcasted_iota(jnp.int32, (CHUNK, cj, ci), 1)

    def spread_edge(q, cols_in):
        turned = lax.broadcasted_iota(jnp.int32, (ci, cells), 0)
        both = jnp.where(turned == 0, cols_in[0, pl.ds(q, 1), :], cols_in[1, pl.ds(q, 1), :])
        edge[q] = both.T

    def around(x, q, c, rows_in):
        start = pl.multiple_of(c * span, span)
        level = pl.ds(pl.multiple_of(c * CHUNK, CHUNK), CHUNK)
        side = edge[q, pl.ds(start, span), :].reshape(CHUNK, cj, ci)
        west = jnp.where(lane == 0, side, pltpu.roll(x, 1, 2))
        east = jnp.where(lane == ci - 1, side, pltpu.roll(x, ci - 1, 2))
        north = jnp.where(row == 0, rows_in[0, q, level, :][:, None, :], pltpu.roll(x, 1, 1))
        south = jnp.where(
            row == cj - 1, rows_in[1, q, level, :][:, None, :], pltpu.roll(x, cj - 1, 1)
        )
        return west, east, north, south

    def couple(c, carry):
        start = pl.multiple_of(c * span, span)
        x = wetp[pl.ds(pl.multiple_of(cj + start, cj), span), :].reshape(CHUNK, cj, ci)
        for n, beside in enumerate(around(x, 2, c, row_recv)):
            coef[n, pl.ds(start, span), :] = (mixing_rate * (x * beside)).reshape(span, ci)
        return carry

    def spread(sources, offset, rows_in, c):
        start = pl.multiple_of(c * span, span)
        weights = [coef[n, pl.ds(start, span), :].reshape(CHUNK, cj, ci) for n in range(4)]
        for q in range(2):
            x = sources[q][pl.ds(start, span), :].reshape(CHUNK, cj, ci)
            total = x
            for weight, beside in zip(weights, around(x, q, c, rows_in)):
                total = total + weight * (beside - x)
            mid[q, pl.ds(pl.multiple_of(cj + start, cj), span), :] = total.reshape(span, ci)

    def mix(c, targets_of):
        start = pl.multiple_of(c * span, span)
        up = pl.ds(start, span)
        here = pl.ds(pl.multiple_of(start + cj, cj), span)
        down = pl.ds(pl.multiple_of(start + 2 * cj, cj), span)
        rate = jnp.broadcast_to(vmix[...][None], (CHUNK, cj, ci)).reshape(span, ci)
        wet_here = rate * wetp[here, :]
        link_up = wet_here * wetp[up, :]
        link_down = wet_here * wetp[down, :]
        for q in range(2):
            x = mid[q, here, :]
            targets_of[q][pl.ds(start, span), :] = (
                x + link_down * (mid[q, down, :] - x) - link_up * (x - mid[q, up, :])
            )

    wet_top = wetp[pl.ds(cj, cj), :]

    def surface():
        link = vmix[...] * wet_top * wetp[pl.ds(2 * cj, cj), :]
        top = []
        for q in range(2):
            x = mid[q, pl.ds(cj, cj), :]
            top.append(x + link * (mid[q, pl.ds(2 * cj, cj), :] - x))
        heat, saltf, base_temp = shelf_melt(top[0], top[1], fric[...], pres[...], wet_top)
        return (
            top[0] - relax_rate * heat,
            top[1] - relax_rate * saltf,
            heat / latent_ratio,
            base_temp,
        )

    def loop(low_c, high_c, body):
        def wrapped(c, carry):
            body(c)
            return carry

        lax.fori_loop(low_c, high_c, wrapped, 0)

    halo_wait(halo1)
    for q in range(3):
        spread_edge(q, col_recv)
    lax.fori_loop(0, chunks, couple, 0)
    loop(0, chunks, functools.partial(spread, (temp, salt), 0, row_recv))
    end_stage(chains[2], 0)
    loop(0, chunks, lambda c: mix(c, (first.at[0], first.at[1])))
    top_temp, top_salt, melt_one, base_one = surface()
    first[0, pl.ds(0, cj), :] = top_temp
    first[1, pl.ds(0, cj), :] = top_salt
    for q in range(2):
        pack(q, first.at[q], 0, row_send2, col_send2)
    halo2 = halo(1, row_send2, row_recv2, col_send2, col_recv2)
    halo_start(halo2)

    groups = enth.shape[1] // width
    for g in range(groups):
        values[pl.ds(g * layers, layers), :] = enth[:, g * width : (g + 1) * width]

    def rate_of(k):
        return jnp.where(k < trans[...], cold_rate, temperate_rate).astype(jnp.float32)

    def layer(k):
        return pl.ds(k, groups, stride=layers)

    def eliminate(k, carry):
        ratio, value, rate, inner_up = carry
        rate_next = rate_of(k + 1)
        inner = 0.5 * (rate + rate_next)
        pivot = 1.0 / (1.0 + inner_up + inner + inner_up * ratio)
        value = (values[layer(k), :] + inner_up * value) * pivot
        ratio = -inner * pivot
        values[layer(k), :] = value
        ratios[pl.ds(pl.multiple_of(k * groups, groups), groups), :] = ratio
        return ratio, value, rate_next, inner

    end_stage(chains[2], 1)
    rate_top = rate_of(0)
    rate_next = rate_of(1)
    inner = 0.5 * (rate_top + rate_next)
    pivot = 1.0 / (1.0 + rate_top + inner)
    value = (values[layer(0), :] + rate_top * surf[...]) * pivot
    ratio = -inner * pivot
    values[layer(0), :] = value
    ratios[pl.ds(0, groups), :] = ratio
    half = layers // 2
    state = lax.fori_loop(1, half, eliminate, (ratio, value, rate_next, inner))

    end_stage(chains[2], 2)
    halo_wait(halo2)
    for q in range(2):
        spread_edge(q, col_recv2)
    second = functools.partial(spread, (first.at[0], first.at[1]), 0, row_recv2)
    second(0)
    top_temp, top_salt, melt_two, base_two = surface()
    mean_melt = 0.5 * (melt_one + melt_two)
    mean_base = 0.5 * (base_one + base_two)

    part = 64

    def pairs(i, carry):
        at = pl.ds(pl.multiple_of(i * part, part), part)
        place = pcol[at, :]
        place_row = place // ci
        place_col = place - place_row * ci
        weight = pw[at, :]
        for slot, table in ((0, mean_melt), (1, mean_base)):
            found = jnp.zeros((part, width), jnp.float32)
            for r in range(cj):
                line = jnp.broadcast_to(table[r : r + 1], (part, ci))
                there = jnp.take_along_axis(
                    line, place_col, axis=1, mode="promise_in_bounds"
                )
                found = jnp.where(place_row == r, there, found)
            high, low = split_two(weight * found)
            pay[slot, at, pl.ds(0, width)] = high
            pay[slot, at, pl.ds(width, width)] = low
        return carry

    lax.fori_loop(0, blocks // part, pairs, 0)
    for slot in range(2):
        sum_blocks(slot, slot, chains[slot][1][0])
        start_stage(chains[slot], 0)

    state_box = [state]

    def rest_spread():
        loop(1, chunks, second)

    def rest_mix():
        loop(0, chunks, lambda c: mix(c, (out_temp, out_salt)))
        out_temp[pl.ds(0, cj), :] = top_temp
        out_salt[pl.ds(0, cj), :] = top_salt

    def rest_eliminate():
        state_box[0] = lax.fori_loop(half, layers - 1, eliminate, state_box[0])

    fill = [rest_spread, rest_mix, rest_eliminate]
    stages = len(orders[0])
    cover_stage = 3
    for stage in range(stages):
        if stage < len(fill):
            fill[stage]()
        end_stage(chains[0], stage)
        end_stage(chains[1], stage)
        if cover_stage < stages:
            end_stage(chains[2], cover_stage)
            cover_stage += 1
    for work in fill[stages:]:
        work()

    share = 1.0 / area[...]
    melt_sum = chains[0][1][-1][...] * share
    base_sum = chains[1][1][-1][...] * share
    cover_sum = chains[2][1][-1][...] * share
    out_melt[...] = melt_sum
    ratio, value, rate, inner_up = state_box[0]
    last = layers - 1
    pivot = 1.0 / (1.0 + inner_up + cover_sum + inner_up * ratio)
    solved = (values[layer(last), :] + base_sum + inner_up * value) * pivot
    values[layer(last), :] = solved

    def substitute(n, below):
        k = last - 1 - n
        solved = values[layer(k), :] - ratios[
            pl.ds(pl.multiple_of(k * groups, groups), groups), :
        ] * below
        values[layer(k), :] = solved
        return solved

    lax.fori_loop(0, last, substitute, solved)
    for g in range(groups):
        out_enth[:, g * width : (g + 1) * width] = values[pl.ds(g * layers, layers), :]

    halo_done(halo1)
    halo_done(halo2)
    for chain in chains:
        drain(chain)


def local(
    nx,
    ny,
    ocean_temp,
    ocean_salt,
    wet_mask,
    vertical_mix,
    friction,
    pressure,
    pair_column,
    pair_weight,
    block_owner,
    block_target,
    enthalpy,
    surface_enthalpy,
    transition_layer,
    column_area,
):
    levels, cj, ci = wet_mask.shape
    cells = levels * cj
    blocks, width = pair_column.shape
    layers, columns = enthalpy.shape
    targets = columns // width
    orders = stage_orders(nx, ny)
    owner = block_owner[:, 0]
    segs = [
        (slot_of(owner, order, ny) * targets + block_target).reshape(1, blocks)
        for order in orders
    ]
    f32 = jnp.float32
    total = nx * ny * targets
    scratch = [
        pltpu.VMEM((cells + 2 * cj, ci), f32),
        pltpu.VMEM((4, cells, ci), f32),
        pltpu.VMEM((2, cells + 2 * cj, ci), f32),
        pltpu.VMEM((3, cells, ci), f32),
        pltpu.VMEM((2, cells, ci), f32),
        pltpu.VMEM((2, 3, levels, ci), f32),
        pltpu.VMEM((2, 3, levels, ci), f32),
        pltpu.VMEM((2, 8, cells), f32),
        pltpu.VMEM((2, 8, cells), f32),
        pltpu.VMEM((2, 2, levels, ci), f32),
        pltpu.VMEM((2, 2, levels, ci), f32),
        pltpu.VMEM((2, 8, cells), f32),
        pltpu.VMEM((2, 8, cells), f32),
        pltpu.VMEM((2, total, blocks), jnp.bfloat16),
        pltpu.VMEM((3, blocks, 2 * width), jnp.bfloat16),
        pltpu.VMEM((layers * targets, width), f32),
        pltpu.VMEM((layers * targets, width), f32),
    ]
    for order in (orders[0], orders[1], orders[0]):
        rows = live_rows(order, total)
        scratch += [pltpu.VMEM((n, width), f32) for n in rows]
        scratch += [
            pltpu.VMEM((radix - 1, n, width), f32)
            for (_, _, radix), n in zip(order, rows[1:])
        ]
        most = max(radix for _, _, radix in order) - 1
        scratch += [pltpu.SemaphoreType.DMA((len(order), most))] * 2
    scratch += [pltpu.SemaphoreType.DMA((2, 4))] * 2
    vmem = pl.BlockSpec(memory_space=pltpu.VMEM)
    sizes = (nx, ny, levels, cj, ci, targets, layers)
    new_temp, new_salt, new_enthalpy, ice_melt = pl.pallas_call(
        functools.partial(kernel, sizes, orders),
        out_shape=(
            jax.ShapeDtypeStruct((cells, ci), f32),
            jax.ShapeDtypeStruct((cells, ci), f32),
            jax.ShapeDtypeStruct((layers, columns), f32),
            jax.ShapeDtypeStruct((targets, width), f32),
        ),
        in_specs=[vmem] * 14,
        out_specs=(vmem,) * 4,
        scratch_shapes=scratch,
        compiler_params=pltpu.CompilerParams(
            collective_id=0, has_side_effects=True, vmem_limit_bytes=48 * 1024 * 1024
        ),
    )(
        ocean_temp.reshape(cells, ci),
        ocean_salt.reshape(cells, ci),
        wet_mask.reshape(cells, ci),
        vertical_mix,
        friction,
        pressure,
        pair_column,
        pair_weight,
        segs[0],
        segs[1],
        enthalpy,
        surface_enthalpy.reshape(targets, width),
        transition_layer.reshape(targets, width),
        column_area.reshape(targets, width),
    )
    return (
        new_temp.reshape(levels, cj, ci),
        new_salt.reshape(levels, cj, ci),
        new_enthalpy,
        ice_melt.reshape(columns),
    )


def solution(mesh):
    return jax.shard_map(
        functools.partial(local, mesh.shape["gx"], mesh.shape["gy"]),
        mesh=mesh,
        in_specs=(
            P(None, "gy", "gx"),
            P(None, "gy", "gx"),
            P(None, "gy", "gx"),
            P("gy", "gx"),
            P("gy", "gx"),
            P("gy", "gx"),
            P(("gx", "gy"), None),
            P(("gx", "gy"), None),
            P(("gx", "gy"), None),
            P(("gx", "gy")),
            P(None, ("gx", "gy")),
            P(("gx", "gy")),
            P(("gx", "gy")),
            P(("gx", "gy")),
        ),
        out_specs=(
            P(None, "gy", "gx"),
            P(None, "gy", "gx"),
            P(None, ("gx", "gy")),
            P(("gx", "gy")),
        ),
        check_vma=False,
    )
```

time: 752 us -> 53.5 us (0.07)
  local copies, waits for them, and re-layouts: 638 us -> 10.8 us
  waiting for transfers between devices: 44.6 us -> 0 us
  Pallas kernels: 0 us -> 40.7 us
  starting transfers between devices: 37.5 us -> 0 us
  other arithmetic: 24.2 us -> 0.75 us
    gather x2 -> x0, local copies, waits for them, and re-layouts: 521 us -> none  [the longest x1 261 us: local(): mean_base[pair_column]]
    dynamic_update_slice x120 -> x0, local copies, waits for them, and re-layouts: 47.2 us -> none  [solve_columns(): lax.scan(forward, start, (diagonal, below, above, right_side))]
    pallas_call x0 -> x1, Pallas kernels: none -> 40.7 us  [local(): pl.pallas_call(functools.partial(kernel, sizes, orders), out_shape=(jax.S...]
    dynamic_slice x120 -> x0, local copies, waits for them, and re-layouts: 39.9 us -> none  [solve_columns(): lax.scan(forward, start, (diagonal, below, above, right_side))]
    all_to_all x2 -> x0, waiting for transfers between devices: 31.1 us -> none  [the longest x1 31.1 us: local(): lax.all_to_all(send_values.reshape(devices, capacity, 3, block_width), ('...]
    ppermute x8 -> x0, starting transfers between devices: 23.1 us -> none  [the longest x4 17.8 us: padded(): lax.ppermute(lax.slice_in_dim(block, block.shape[dim] - width, None, axis...]
    scatter x2 -> x0, local copies, waits for them, and re-layouts: 16 us -> none  [the longest x1 13.6 us: local(): jnp.zeros((devices * capacity, 3, block_width), jnp.float32).at[slot]]
    all_to_all x2 -> x0, starting transfers between devices: 14.4 us -> none  [the longest x1 8.02 us: local(): lax.all_to_all(send_values.reshape(devices, capacity, 3, block_width), ('...]
  transfers between devices with their start and end apart: 10 -> 0, of which waited for: 2 -> 0; matrix products, arithmetic and copies ran while one was open for 75% -> 0% of each run, Pallas kernels for 0% -> 0%
where the time goes in v1:
time: 53.5 us; the launch traced here: 53 us
  Pallas kernels  40.7 us (76%)
  local copies, waits for them, and re-layouts  10.8 us (20%)
  other arithmetic  0.75 us (1%)
  between operations  0.71 us (1%)
    pallas_call x1, Pallas kernels, local(): pl.pallas_call(functools.partial(kernel, sizes, orders), out_shape=(jax.S...  40.7 us
    unnamed x28, local copies, waits for them, and re-layouts  10.8 us

profile of v1, /device:TPU:0, one launch (start us, length us, event | category | flops | bytes accessed | tf_op | source)
XLA Modules:
  0.0 53.0 jit_solution(15179966830052812028)
XLA Ops:
  0.6 0.0 copy-start.6
  0.6 0.0 copy-start.10
  0.7 0.0 copy-start.11
  0.7 0.7 %multiply_add_fusion = (s32[512]{0:T(512)S(1)}, s32[512]{0:T(512)S(1)}) fusion(s32[512]{0:T(512)} %param.23, s32[512]{0:T(512)} %bitcast.23), kind=kLoop, calls=%fused_computation.32 | loop fusion | flops 60928 | bytes 8192 | tf_op jit(solution)/shard_map/add | solution.py:527
  1.4 0.0 copy-start.9
  1.4 0.0 copy-done.6
  1.4 0.0 copy-done.10
  1.4 0.0 copy-done.11
  1.5 0.6 %copy-done.9 = f32[8,128]{1,0:T(8,128)S(1)} copy-done((f32[8,128]{1,0:T(8,128)S(1)}, f32[8,128]{1,0:T(8,128)}, u32[]{:S(2)}) %copy-start.9) | copy-done | bytes 4120
  2.1 0.0 copy-start
  2.1 1.1 %copy-done = f32[40,4096]{1,0:T(8,128)S(1)} copy-done((f32[40,4096]{1,0:T(8,128)S(1)}, f32[40,4096]{1,0:T(8,128)}, u32[]{:S(2)}) %copy-start) | copy-done | bytes 655384
  3.2 0.0 copy-start.1
  3.2 0.9 %copy-done.1 = f32[64,8,128]{2,1,0:T(8,128)S(1)} copy-done((f32[64,8,128]{2,1,0:T(8,128)S(1)}, f32[64,8,128]{2,1,0:T(8,128)}, u32[]{:S(2)}) %copy-start.1) | copy-done | bytes 262168
  4.1 0.0 copy-start.2
  4.1 0.9 %copy-done.2 = f32[64,8,128]{2,1,0:T(8,128)S(1)} copy-done((f32[64,8,128]{2,1,0:T(8,128)S(1)}, f32[64,8,128]{2,1,0:T(8,128)}, u32[]{:S(2)}) %copy-start.2) | copy-done | bytes 262168
  5.1 0.0 copy-start.3
  5.1 0.9 %copy-done.3 = s32[64,8,128]{2,1,0:T(8,128)S(1)} copy-done((s32[64,8,128]{2,1,0:T(8,128)S(1)}, s32[64,8,128]{2,1,0:T(8,128)}, u32[]{:S(2)}) %copy-start.3) | copy-done | bytes 262168
  6.0 0.0 copy-start.4
  6.0 0.9 %copy-done.4 = s32[512,128]{1,0:T(8,128)S(1)} copy-done((s32[512,128]{1,0:T(8,128)S(1)}, s32[512,128]{1,0:T(8,128)}, u32[]{:S(2)}) %copy-start.4) | copy-done | bytes 262168
  7.0 0.0 copy-start.5
  7.0 0.9 %copy-done.5 = f32[512,128]{1,0:T(8,128)S(1)} copy-done((f32[512,128]{1,0:T(8,128)S(1)}, f32[512,128]{1,0:T(8,128)}, u32[]{:S(2)}) %copy-start.5) | copy-done | bytes 262168
  7.9 0.0 copy-start.7
  7.9 0.7 %copy-done.7 = s32[4096]{0:T(1024)S(1)} copy-done((s32[4096]{0:T(1024)S(1)}, s32[4096]{0:T(1024)}, u32[]{:S(2)}) %copy-start.7) | copy-done | bytes 16408
  8.7 0.0 copy-start.8
  8.7 0.7 %copy-done.8 = f32[4096]{0:T(1024)S(1)} copy-done((f32[4096]{0:T(1024)S(1)}, f32[4096]{0:T(1024)}, u32[]{:S(2)}) %copy-start.8) | copy-done | bytes 16408
  9.4 40.7 %shard_map.165 = (f32[512,128]{1,0:T(8,128)S(1)}, f32[512,128]{1,0:T(8,128)S(1)}, f32[40,4096]{1,0:T(8,128)S(1)}, f32[32,128]{1,0:T(8,128)S(1)}) custom-call(f32[512,128]{1,0:T(8,128)S(1)} %bitcast.14, f32[512,128]{1,0:T(8,128)S(1)} %bitcast.15, s32[512,128]{1,0:T(8,128)S(1)} %bitcast.16, f32[8,128]{1,0:T(8,128)S(1)} %copy-done.9, f32[8,128]{1,0:T(8,128)S(1)} %copy-done.10, ...), custom_call_target="tpu_custom_call" | custom-call | tf_op jit(solution)/shard_map/pallas_call | solution.py:563
  50.1 0.7 %copy.22 = f32[64,8,128]{2,1,0:T(8,128)} copy(f32[64,8,128]{2,1,0:T(8,128)S(1)} %bitcast.13) | data formatting | bytes 524288
  50.8 0.7 %copy.23 = f32[64,8,128]{2,1,0:T(8,128)} copy(f32[64,8,128]{2,1,0:T(8,128)S(1)} %bitcast.12) | data formatting | bytes 524288
  51.5 0.8 %copy.24 = f32[40,4096]{1,0:T(8,128)} copy(f32[40,4096]{1,0:T(8,128)S(1)} %get-tuple-element.20) | data formatting | bytes 1310720
  52.4 0.6 %copy.25 = f32[4096]{0:T(1024)} copy(f32[4096]{0:T(1024)S(1)} %bitcast.20) | data formatting | bytes 32768
Async XLA Ops:
  0.6 0.8 %copy-start.6 = (f32[4096]{0:T(1024)S(1)}, f32[4096]{0:T(1024)}, u32[]{:S(2)}) copy-start(f32[4096]{0:T(1024)} %param.25) | copy-start | bytes 49156
  0.6 0.8 %copy-start.10 = (f32[8,128]{1,0:T(8,128)S(1)}, f32[8,128]{1,0:T(8,128)}, u32[]{:S(2)}) copy-start(f32[8,128]{1,0:T(8,128)} %refs_4_.1) | copy-start | bytes 12292
  0.7 0.8 %copy-start.11 = (f32[8,128]{1,0:T(8,128)S(1)}, f32[8,128]{1,0:T(8,128)}, u32[]{:S(2)}) copy-start(f32[8,128]{1,0:T(8,128)} %refs_5_.1) | copy-start | bytes 12292
  1.4 0.7 %copy-start.9 = (f32[8,128]{1,0:T(8,128)S(1)}, f32[8,128]{1,0:T(8,128)}, u32[]{:S(2)}) copy-start(f32[8,128]{1,0:T(8,128)} %refs_3_.1) | copy-start | bytes 12292
  2.1 1.1 %copy-start = (f32[40,4096]{1,0:T(8,128)S(1)}, f32[40,4096]{1,0:T(8,128)}, u32[]{:S(2)}) copy-start(f32[40,4096]{1,0:T(8,128)} %refs_10_.1) | copy-start | bytes 1966084
  3.2 0.9 %copy-start.1 = (f32[64,8,128]{2,1,0:T(8,128)S(1)}, f32[64,8,128]{2,1,0:T(8,128)}, u32[]{:S(2)}) copy-start(f32[64,8,128]{2,1,0:T(8,128)} %param.14) | copy-start | bytes 786436
  4.1 0.9 %copy-start.2 = (f32[64,8,128]{2,1,0:T(8,128)S(1)}, f32[64,8,128]{2,1,0:T(8,128)}, u32[]{:S(2)}) copy-start(f32[64,8,128]{2,1,0:T(8,128)} %param.15) | copy-start | bytes 786436
  5.1 0.9 %copy-start.3 = (s32[64,8,128]{2,1,0:T(8,128)S(1)}, s32[64,8,128]{2,1,0:T(8,128)}, u32[]{:S(2)}) copy-start(s32[64,8,128]{2,1,0:T(8,128)} %param.16) | copy-start | bytes 786436
  6.0 0.9 %copy-start.4 = (s32[512,128]{1,0:T(8,128)S(1)}, s32[512,128]{1,0:T(8,128)}, u32[]{:S(2)}) copy-start(s32[512,128]{1,0:T(8,128)} %refs_6_.1) | copy-start | bytes 786436
  7.0 0.9 %copy-start.5 = (f32[512,128]{1,0:T(8,128)S(1)}, f32[512,128]{1,0:T(8,128)}, u32[]{:S(2)}) copy-start(f32[512,128]{1,0:T(8,128)} %refs_7_.1) | copy-start | bytes 786436
  7.9 0.7 %copy-start.7 = (s32[4096]{0:T(1024)S(1)}, s32[4096]{0:T(1024)}, u32[]{:S(2)}) copy-start(s32[4096]{0:T(1024)} %param.26) | copy-start | bytes 49156
  8.7 0.7 %copy-start.8 = (f32[4096]{0:T(1024)S(1)}, f32[4096]{0:T(1024)}, u32[]{:S(2)}) copy-start(f32[4096]{0:T(1024)} %param.27) | copy-start | bytes 49156

commit v2 on v1

--- a/solution.py
+++ b/solution.py
@@ -19,6 +19,7 @@
 
 MESH = pl.DeviceIdType.MESH
 CHUNK = 8
+LIMIT = 62 * 1024 * 1024
 
 
 def shelf_melt(surface_temp, surface_salt, friction, pressure, wet_top):
@@ -45,6 +46,8 @@
     base = 1
     while size > 1:
         radix = next(p for p in range(2, size + 1) if size % p == 0)
+        if axis == "gx" and size == 4:
+            radix = size
         found.append((axis, base, radix))
         base *= radix
         size //= radix
@@ -89,11 +92,28 @@
         del refs[:count]
         return out
 
-    (temp, salt, wet, vmix, fric, pres, pcol, pw, seg_a, seg_b, enth, surf, trans, area) = take(14)
-    (out_temp, out_salt, out_enth, out_melt) = take(4)
+    given = take(14)
+    results = take(4)
+    held = take(14)
+    (out_temp, out_salt, out_enth, out_melt) = made = take(4)
+    (load_sem, save_sem) = take(2)
+    saves = [
+        pltpu.make_async_copy(src, dst, save_sem.at[i])
+        for i, (src, dst) in enumerate(zip(made, results))
+    ]
+    loads = [
+        pltpu.make_async_copy(src, dst, load_sem.at[i])
+        for i, (src, dst) in enumerate(zip(given, held))
+    ]
+    for load in loads:
+        load.start()
+    (temp, salt, wet, vmix, fric, pres, owner, target, pw, trans, surf, enth, pcol, area) = held
     (wetp, coef, mid, edge, first) = take(5)
+    (edge_top, first_top, last_layer) = take(3)
     (row_send, row_recv, col_send, col_recv) = take(4)
     (row_send2, row_recv2, col_send2, col_recv2) = take(4)
+    (row_top, row_top_in, col_top, col_top_in) = take(4)
+    (row_top2, row_top_in2, col_top2, col_top_in2) = take(4)
     (hot, pay, ratios, values) = take(4)
     chains = []
     for order in (orders[0], orders[1], orders[0]):
@@ -119,12 +139,12 @@
         (gx < nx - 1, {"gx": gx + 1}),
     )
 
-    for buf in (row_recv, row_recv2):
+    for buf in (row_recv, row_recv2, row_top_in, row_top_in2):
         for side in range(2):
             @pl.when(jnp.logical_not(sides[side][0]))
             def _():
                 buf[side] = jnp.zeros(buf.shape[1:], jnp.float32)
-    for buf in (col_recv, col_recv2):
+    for buf in (col_recv, col_recv2, col_top_in, col_top_in2):
         for side in range(2):
             @pl.when(jnp.logical_not(sides[2 + side][0]))
             def _():
@@ -147,24 +167,31 @@
     zeros_pad = jnp.zeros((cj, ci), jnp.float32)
     wetp[pl.ds(0, cj), :] = zeros_pad
     wetp[pl.ds(cj + cells, cj), :] = zeros_pad
-    wetp[pl.ds(cj, cells), :] = wet[...].astype(jnp.float32)
     for q in range(2):
         mid[q, pl.ds(0, cj), :] = zeros_pad
         mid[q, pl.ds(cj + cells, cj), :] = zeros_pad
 
     def pack(q, source, offset, rows, cols):
-        rows[0, q] = source[pl.ds(offset, levels, stride=cj), :]
-        rows[1, q] = source[pl.ds(offset + cj - 1, levels, stride=cj), :]
-        turned = source[pl.ds(offset, cells), :].T
+        count = rows.shape[2]
+        rows[0, q] = source[pl.ds(offset, count, stride=cj), :]
+        rows[1, q] = source[pl.ds(offset + cj - 1, count, stride=cj), :]
+        turned = source[pl.ds(offset, cols.shape[2]), :].T
         cols[0, pl.ds(q, 1), :] = turned[0:1]
         cols[1, pl.ds(q, 1), :] = turned[ci - 1 : ci]
 
-    for cols in (col_send, col_send2):
+    for cols in (col_send, col_send2, col_top, col_top2):
         cols[...] = jnp.zeros(cols.shape, jnp.float32)
-    pack(0, temp, 0, row_send, col_send)
-    pack(1, salt, 0, row_send, col_send)
-    pack(2, wetp, cj, row_send, col_send)
-
+    first_top[...] = jnp.zeros(first_top.shape, jnp.float32)
+    for load in loads[:3]:
+        load.wait()
+    wetp[pl.ds(cj, cells), :] = wet[...].astype(jnp.float32)
+
+    def pack_all(rows, cols):
+        pack(0, temp, 0, rows, cols)
+        pack(1, salt, 0, rows, cols)
+        pack(2, wetp, cj, rows, cols)
+
+    pack_all(row_top, col_top)
     pl.semaphore_wait(barrier, partners)
 
     def halo(step, rows, rows_in, cols, cols_in):
@@ -203,6 +230,9 @@
             def _():
                 copy.wait_send()
 
+    halo_top1 = halo(2, row_top, row_top_in, col_top, col_top_in)
+    halo_start(halo_top1)
+    pack_all(row_send, col_send)
     halo1 = halo(0, row_send, row_recv, col_send, col_recv)
     halo_start(halo1)
 
@@ -250,13 +280,15 @@
                 copy.wait_send()
 
     seg_total = chains[0][1][0].shape[0]
-    hot_rows = 256
-
-    def build_hot(which, seg):
+    hot_rows = min(256, seg_total)
+
+    def build_hot(which):
+        seg = slot_of(owner[...], orders[which], ny) * targets + target[...]
+
         def body(i, carry):
             start = pl.multiple_of(i * hot_rows, hot_rows)
             row = lax.broadcasted_iota(jnp.int32, (hot_rows, blocks), 0) + start
-            hit = (row == seg[...]).astype(jnp.float32)
+            hit = (row == seg).astype(jnp.float32)
             hot[which, pl.ds(start, hot_rows), :] = hit.astype(jnp.bfloat16)
             return carry
 
@@ -275,23 +307,26 @@
 
         lax.fori_loop(0, seg_total // hot_rows, body, 0)
 
-    build_hot(0, seg_a)
+    for load in loads[6:9]:
+        load.wait()
+    build_hot(0)
     high, low = split_two(pw[...])
     pay[2, :, pl.ds(0, width)] = high
     pay[2, :, pl.ds(width, width)] = low
     sum_blocks(0, 2, chains[2][1][0])
     start_stage(chains[2], 0)
-    build_hot(1, seg_b)
+    for load in loads[3:6]:
+        load.wait()
 
     lane = lax.broadcasted_iota(jnp.int32, (CHUNK, cj, ci), 2)
     row = lax.broadcasted_iota(jnp.int32, (CHUNK, cj, ci), 1)
 
-    def spread_edge(q, cols_in):
-        turned = lax.broadcasted_iota(jnp.int32, (ci, cells), 0)
+    def spread_edge(q, cols_in, edge):
+        turned = lax.broadcasted_iota(jnp.int32, (ci, cols_in.shape[2]), 0)
         both = jnp.where(turned == 0, cols_in[0, pl.ds(q, 1), :], cols_in[1, pl.ds(q, 1), :])
         edge[q] = both.T
 
-    def around(x, q, c, rows_in):
+    def around(x, q, c, rows_in, edge):
         start = pl.multiple_of(c * span, span)
         level = pl.ds(pl.multiple_of(c * CHUNK, CHUNK), CHUNK)
         side = edge[q, pl.ds(start, span), :].reshape(CHUNK, cj, ci)
@@ -303,20 +338,19 @@
         )
         return west, east, north, south
 
-    def couple(c, carry):
+    def couple(rows_in, edge, c):
         start = pl.multiple_of(c * span, span)
         x = wetp[pl.ds(pl.multiple_of(cj + start, cj), span), :].reshape(CHUNK, cj, ci)
-        for n, beside in enumerate(around(x, 2, c, row_recv)):
+        for n, beside in enumerate(around(x, 2, c, rows_in, edge)):
             coef[n, pl.ds(start, span), :] = (mixing_rate * (x * beside)).reshape(span, ci)
-        return carry
-
-    def spread(sources, offset, rows_in, c):
+
+    def spread(sources, rows_in, edge, c):
         start = pl.multiple_of(c * span, span)
         weights = [coef[n, pl.ds(start, span), :].reshape(CHUNK, cj, ci) for n in range(4)]
         for q in range(2):
             x = sources[q][pl.ds(start, span), :].reshape(CHUNK, cj, ci)
             total = x
-            for weight, beside in zip(weights, around(x, q, c, rows_in)):
+            for weight, beside in zip(weights, around(x, q, c, rows_in, edge)):
                 total = total + weight * (beside - x)
             mid[q, pl.ds(pl.multiple_of(cj + start, cj), span), :] = total.reshape(span, ci)
 
@@ -358,21 +392,24 @@
 
         lax.fori_loop(low_c, high_c, wrapped, 0)
 
-    halo_wait(halo1)
+    halo_wait(halo_top1)
     for q in range(3):
-        spread_edge(q, col_recv)
-    lax.fori_loop(0, chunks, couple, 0)
-    loop(0, chunks, functools.partial(spread, (temp, salt), 0, row_recv))
+        spread_edge(q, col_top_in, edge_top)
+    couple(row_top_in, edge_top, 0)
+    spread((temp, salt), row_top_in, edge_top, 0)
+    mix(0, (first_top.at[0], first_top.at[1]))
+    top_temp, top_salt, melt_one, base_one = surface()
+    first_top[0, pl.ds(0, cj), :] = top_temp
+    first_top[1, pl.ds(0, cj), :] = top_salt
+    for q in range(2):
+        pack(q, first_top.at[q], 0, row_top2, col_top2)
+    halo_top2 = halo(3, row_top2, row_top_in2, col_top2, col_top_in2)
+    halo_start(halo_top2)
+
+    build_hot(1)
     end_stage(chains[2], 0)
-    loop(0, chunks, lambda c: mix(c, (first.at[0], first.at[1])))
-    top_temp, top_salt, melt_one, base_one = surface()
-    first[0, pl.ds(0, cj), :] = top_temp
-    first[1, pl.ds(0, cj), :] = top_salt
-    for q in range(2):
-        pack(q, first.at[q], 0, row_send2, col_send2)
-    halo2 = halo(1, row_send2, row_recv2, col_send2, col_recv2)
-    halo_start(halo2)
-
+    for load in loads[9:12]:
+        load.wait()
     groups = enth.shape[1] // width
     for g in range(groups):
         values[pl.ds(g * layers, layers), :] = enth[:, g * width : (g + 1) * width]
@@ -391,10 +428,9 @@
         value = (values[layer(k), :] + inner_up * value) * pivot
         ratio = -inner * pivot
         values[layer(k), :] = value
-        ratios[pl.ds(pl.multiple_of(k * groups, groups), groups), :] = ratio
+        ratios[layer(k), :] = ratio
         return ratio, value, rate_next, inner
 
-    end_stage(chains[2], 1)
     rate_top = rate_of(0)
     rate_next = rate_of(1)
     inner = 0.5 * (rate_top + rate_next)
@@ -402,19 +438,19 @@
     value = (values[layer(0), :] + rate_top * surf[...]) * pivot
     ratio = -inner * pivot
     values[layer(0), :] = value
-    ratios[pl.ds(0, groups), :] = ratio
-    half = layers // 2
-    state = lax.fori_loop(1, half, eliminate, (ratio, value, rate_next, inner))
-
-    end_stage(chains[2], 2)
-    halo_wait(halo2)
+    ratios[layer(0), :] = ratio
+    last = layers - 1
+    state = lax.fori_loop(1, last, eliminate, (ratio, value, rate_next, inner))
+
+    halo_wait(halo_top2)
     for q in range(2):
-        spread_edge(q, col_recv2)
-    second = functools.partial(spread, (first.at[0], first.at[1]), 0, row_recv2)
-    second(0)
-    top_temp, top_salt, melt_two, base_two = surface()
+        spread_edge(q, col_top_in2, edge_top)
+    spread((first_top.at[0], first_top.at[1]), row_top_in2, edge_top, 0)
+    new_top_temp, new_top_salt, melt_two, base_two = surface()
     mean_melt = 0.5 * (melt_one + melt_two)
     mean_base = 0.5 * (base_one + base_two)
+    for load in loads[12:]:
+        load.wait()
 
     part = 64
 
@@ -442,30 +478,71 @@
         sum_blocks(slot, slot, chains[slot][1][0])
         start_stage(chains[slot], 0)
 
-    state_box = [state]
-
-    def rest_spread():
-        loop(1, chunks, second)
-
-    def rest_mix():
+    halo2 = halo(1, row_send2, row_recv2, col_send2, col_recv2)
+
+    def first_spread():
+        halo_wait(halo1)
+        for q in range(3):
+            spread_edge(q, col_recv, edge)
+        loop(0, chunks, functools.partial(couple, row_recv, edge))
+        loop(0, chunks, functools.partial(spread, (temp, salt), row_recv, edge))
+
+    def first_mix():
+        loop(0, chunks, lambda c: mix(c, (first.at[0], first.at[1])))
+        first[0, pl.ds(0, cj), :] = top_temp
+        first[1, pl.ds(0, cj), :] = top_salt
+        for q in range(2):
+            pack(q, first.at[q], 0, row_send2, col_send2)
+        halo_start(halo2)
+
+    def second_step():
+        halo_wait(halo2)
+        for q in range(2):
+            spread_edge(q, col_recv2, edge)
+        sources = (first.at[0], first.at[1])
+        loop(0, chunks, functools.partial(spread, sources, row_recv2, edge))
         loop(0, chunks, lambda c: mix(c, (out_temp, out_salt)))
-        out_temp[pl.ds(0, cj), :] = top_temp
-        out_salt[pl.ds(0, cj), :] = top_salt
-
-    def rest_eliminate():
-        state_box[0] = lax.fori_loop(half, layers - 1, eliminate, state_box[0])
-
-    fill = [rest_spread, rest_mix, rest_eliminate]
+        out_temp[pl.ds(0, cj), :] = new_top_temp
+        out_salt[pl.ds(0, cj), :] = new_top_salt
+        saves[0].start()
+        saves[1].start()
+
+    ratio_end, value_end, rate_end, inner_end = state
+
+    def back_terms():
+        ratios[layer(last - 1), :] = -ratio_end
+
+        def body(n, carry):
+            level, slope = carry
+            k = last - 2 - n
+            ratio = ratios[layer(k), :]
+            level = values[layer(k), :] - ratio * level
+            slope = -ratio * slope
+            values[layer(k), :] = level
+            ratios[layer(k), :] = slope
+            return level, slope
+
+        lax.fori_loop(0, last - 1, body, (value_end, -ratio_end))
+        last_side = values[layer(last), :]
+        values[layer(last), :] = jnp.zeros((groups, width), jnp.float32)
+        ratios[layer(last), :] = jnp.ones((groups, width), jnp.float32)
+        return last_side
+
+    side_box = []
+    fill = [
+        first_spread,
+        first_mix,
+        lambda: side_box.append(back_terms()),
+        second_step,
+    ]
     stages = len(orders[0])
-    cover_stage = 3
     for stage in range(stages):
         if stage < len(fill):
             fill[stage]()
         end_stage(chains[0], stage)
         end_stage(chains[1], stage)
-        if cover_stage < stages:
-            end_stage(chains[2], cover_stage)
-            cover_stage += 1
+        if stage + 1 < stages:
+            end_stage(chains[2], stage + 1)
     for work in fill[stages:]:
         work()
 
@@ -474,28 +551,36 @@
     base_sum = chains[1][1][-1][...] * share
     cover_sum = chains[2][1][-1][...] * share
     out_melt[...] = melt_sum
-    ratio, value, rate, inner_up = state_box[0]
-    last = layers - 1
-    pivot = 1.0 / (1.0 + inner_up + cover_sum + inner_up * ratio)
-    solved = (values[layer(last), :] + base_sum + inner_up * value) * pivot
-    values[layer(last), :] = solved
-
-    def substitute(n, below):
-        k = last - 1 - n
-        solved = values[layer(k), :] - ratios[
-            pl.ds(pl.multiple_of(k * groups, groups), groups), :
-        ] * below
-        values[layer(k), :] = solved
-        return solved
-
-    lax.fori_loop(0, last, substitute, solved)
+    pivot = 1.0 / (1.0 + inner_end + cover_sum + inner_end * ratio_end)
+    last_layer[...] = (side_box[0] + base_sum + inner_end * value_end) * pivot
     for g in range(groups):
-        out_enth[:, g * width : (g + 1) * width] = values[pl.ds(g * layers, layers), :]
-
+        rows = pl.ds(g * layers, layers)
+        solved = values[rows, :] + ratios[rows, :] * last_layer[pl.ds(g, 1), :]
+        out_enth[:, g * width : (g + 1) * width] = solved
+    saves[2].start()
+    saves[3].start()
+
+    halo_done(halo_top1)
+    halo_done(halo_top2)
     halo_done(halo1)
     halo_done(halo2)
     for chain in chains:
         drain(chain)
+    for save in saves:
+        save.wait()
+
+
+def store(*refs):
+    count = len(refs) // 2
+    sem = refs[-1]
+    copies = [
+        pltpu.make_async_copy(src, dst, sem.at[i])
+        for i, (src, dst) in enumerate(zip(refs[:count], refs[count:-1]))
+    ]
+    for copy in copies:
+        copy.start()
+    for copy in copies:
+        copy.wait()
 
 
 def local(
@@ -522,19 +607,43 @@
     layers, columns = enthalpy.shape
     targets = columns // width
     orders = stage_orders(nx, ny)
-    owner = block_owner[:, 0]
-    segs = [
-        (slot_of(owner, order, ny) * targets + block_target).reshape(1, blocks)
-        for order in orders
-    ]
     f32 = jnp.float32
     total = nx * ny * targets
-    scratch = [
+    given = (
+        ocean_temp.reshape(cells, ci),
+        ocean_salt.reshape(cells, ci),
+        wet_mask.reshape(cells, ci),
+        vertical_mix,
+        friction,
+        pressure,
+        block_owner.reshape(1, blocks),
+        block_target.reshape(1, blocks),
+        pair_weight,
+        transition_layer.reshape(targets, width),
+        surface_enthalpy.reshape(targets, width),
+        enthalpy,
+        pair_column,
+        column_area.reshape(targets, width),
+    )
+    results = (
+        jax.ShapeDtypeStruct((cells, ci), f32),
+        jax.ShapeDtypeStruct((cells, ci), f32),
+        jax.ShapeDtypeStruct((layers, columns), f32),
+        jax.ShapeDtypeStruct((targets, width), f32),
+    )
+    top_cells = 2 * CHUNK * cj
+    scratch = [pltpu.VMEM(leaf.shape, leaf.dtype) for leaf in given]
+    scratch += [pltpu.VMEM(leaf.shape, leaf.dtype) for leaf in results]
+    scratch += [pltpu.SemaphoreType.DMA((len(given),)), pltpu.SemaphoreType.DMA((4,))]
+    scratch += [
         pltpu.VMEM((cells + 2 * cj, ci), f32),
         pltpu.VMEM((4, cells, ci), f32),
         pltpu.VMEM((2, cells + 2 * cj, ci), f32),
         pltpu.VMEM((3, cells, ci), f32),
         pltpu.VMEM((2, cells, ci), f32),
+        pltpu.VMEM((3, top_cells, ci), f32),
+        pltpu.VMEM((2, top_cells, ci), f32),
+        pltpu.VMEM((targets, width), f32),
         pltpu.VMEM((2, 3, levels, ci), f32),
         pltpu.VMEM((2, 3, levels, ci), f32),
         pltpu.VMEM((2, 8, cells), f32),
@@ -543,6 +652,14 @@
         pltpu.VMEM((2, 2, levels, ci), f32),
         pltpu.VMEM((2, 8, cells), f32),
         pltpu.VMEM((2, 8, cells), f32),
+        pltpu.VMEM((2, 3, CHUNK, ci), f32),
+        pltpu.VMEM((2, 3, CHUNK, ci), f32),
+        pltpu.VMEM((2, 8, top_cells), f32),
+        pltpu.VMEM((2, 8, top_cells), f32),
+        pltpu.VMEM((2, 2, CHUNK, ci), f32),
+        pltpu.VMEM((2, 2, CHUNK, ci), f32),
+        pltpu.VMEM((2, 8, top_cells), f32),
+        pltpu.VMEM((2, 8, top_cells), f32),
         pltpu.VMEM((2, total, blocks), jnp.bfloat16),
         pltpu.VMEM((3, blocks, 2 * width), jnp.bfloat16),
         pltpu.VMEM((layers * targets, width), f32),
@@ -557,39 +674,27 @@
         ]
         most = max(radix for _, _, radix in order) - 1
         scratch += [pltpu.SemaphoreType.DMA((len(order), most))] * 2
-    scratch += [pltpu.SemaphoreType.DMA((2, 4))] * 2
-    vmem = pl.BlockSpec(memory_space=pltpu.VMEM)
+    scratch += [pltpu.SemaphoreType.DMA((4, 4))] * 2
     sizes = (nx, ny, levels, cj, ci, targets, layers)
-    new_temp, new_salt, new_enthalpy, ice_melt = pl.pallas_call(
+    hbm = pl.BlockSpec(memory_space=pltpu.HBM)
+    made = pl.pallas_call(
         functools.partial(kernel, sizes, orders),
-        out_shape=(
-            jax.ShapeDtypeStruct((cells, ci), f32),
-            jax.ShapeDtypeStruct((cells, ci), f32),
-            jax.ShapeDtypeStruct((layers, columns), f32),
-            jax.ShapeDtypeStruct((targets, width), f32),
-        ),
-        in_specs=[vmem] * 14,
-        out_specs=(vmem,) * 4,
+        out_shape=results,
+        in_specs=[hbm] * len(given),
+        out_specs=(hbm,) * 4,
         scratch_shapes=scratch,
         compiler_params=pltpu.CompilerParams(
-            collective_id=0, has_side_effects=True, vmem_limit_bytes=48 * 1024 * 1024
+            collective_id=0, has_side_effects=True, vmem_limit_bytes=LIMIT
         ),
-    )(
-        ocean_temp.reshape(cells, ci),
-        ocean_salt.reshape(cells, ci),
-        wet_mask.reshape(cells, ci),
-        vertical_mix,
-        friction,
-        pressure,
-        pair_column,
-        pair_weight,
-        segs[0],
-        segs[1],
-        enthalpy,
-        surface_enthalpy.reshape(targets, width),
-        transition_layer.reshape(targets, width),
-        column_area.reshape(targets, width),
-    )
+    )(*given)
+    new_temp, new_salt, new_enthalpy, ice_melt = pl.pallas_call(
+        store,
+        out_shape=results,
+        in_specs=[hbm] * 4,
+        out_specs=(hbm,) * 4,
+        scratch_shapes=[pltpu.SemaphoreType.DMA((4,))],
+        compiler_params=pltpu.CompilerParams(vmem_limit_bytes=LIMIT),
+    )(*made)
     return (
         new_temp.reshape(levels, cj, ci),
         new_salt.reshape(levels, cj, ci),

time: 53.5 us -> 72.3 us (1.35)
  Pallas kernels: 40.7 us -> 71.5 us
  local copies, waits for them, and re-layouts: 10.8 us -> 0 us
  other arithmetic: 0.75 us -> 0 us
    pallas_call x1 -> x2, Pallas kernels: 40.7 us -> 71.5 us  [the longest x1 37.4 us: local(): pl.pallas_call(store, out_shape=results, in_specs=[hbm] * 4, out_specs=(h...]
    unnamed x28 -> x0, local copies, waits for them, and re-layouts: 10.8 us -> none
    add x1 -> x0, other arithmetic: 0.75 us -> none  [local(): slot_of(owner, order, ny) * targets + block_target]
where the time goes in v2:
time: 72.3 us; the launch traced here: 72.1 us
  Pallas kernels  71.5 us (99%)
    pallas_call x1, Pallas kernels, local(): pl.pallas_call(store, out_shape=results, in_specs=[hbm] * 4, out_specs=(h...  37.4 us
    pallas_call x1, Pallas kernels, local(): pl.pallas_call(functools.partial(kernel, sizes, orders), out_shape=result...  34.1 us

profile of v2, /device:TPU:0, one launch (start us, length us, event | category | flops | bytes accessed | tf_op | source)
XLA Modules:
  0.0 72.1 jit_solution(13705859309835211055)
XLA Ops:
  0.6 34.1 %shard_map.165 = (f32[512,128]{1,0:T(8,128)}, f32[512,128]{1,0:T(8,128)}, f32[40,4096]{1,0:T(8,128)}, f32[32,128]{1,0:T(8,128)}) custom-call(f32[512,128]{1,0:T(8,128)} %bitcast.11, f32[512,128]{1,0:T(8,128)} %bitcast.12, s32[512,128]{1,0:T(8,128)} %bitcast.13, f32[8,128]{1,0:T(8,128)} %refs_3_.1, f32[8,128]{1,0:T(8,128)} %refs_4_.1, f32[8,128]{1,0:T(8,128)} %refs_5_.1, ...), custom_call_target="tpu_custom_call" | custom-call | tf_op jit(solution)/shard_map/pallas_call | solution.py:680
  34.8 37.4 %shard_map.166 = (f32[512,128]{1,0:T(8,128)}, f32[512,128]{1,0:T(8,128)}, f32[40,4096]{1,0:T(8,128)}, f32[32,128]{1,0:T(8,128)}) custom-call(f32[512,128]{1,0:T(8,128)} %get-tuple-element.12.refs_0_, f32[512,128]{1,0:T(8,128)} %get-tuple-element.13.refs_1_, f32[40,4096]{1,0:T(8,128)} %get-tuple-element.14.refs_2_, f32[32,128]{1,0:T(8,128)} %get-tuple-element.15.refs_3_), custom_call_target="tpu_custom_call" | custom-call | tf_op jit(solution)/shard_map/pallas_call | solution.py:690

commit v3 on v2

--- a/solution.py
+++ b/solution.py
@@ -19,6 +19,7 @@
 
 MESH = pl.DeviceIdType.MESH
 CHUNK = 8
+PARTS = 2
 LIMIT = 62 * 1024 * 1024
 
 
@@ -116,7 +117,7 @@
     (row_top2, row_top_in2, col_top2, col_top_in2) = take(4)
     (hot, pay, ratios, values) = take(4)
     chains = []
-    for order in (orders[0], orders[1], orders[0]):
+    for order in (orders[0], orders[1], orders[0]) * PARTS:
         live = take(len(order) + 1)
         got = take(len(order))
         send_sem, recv_sem = take(2)
@@ -279,11 +280,16 @@
             for copy in make_copies(chain, stage):
                 copy.wait_send()
 
-    seg_total = chains[0][1][0].shape[0]
-    hot_rows = min(256, seg_total)
+    part_rows = chains[0][1][0].shape[0]
+    seg_total = part_rows * PARTS
+    share_rows = targets // PARTS
+    hot_rows = min(256, part_rows)
 
     def build_hot(which):
-        seg = slot_of(owner[...], orders[which], ny) * targets + target[...]
+        place = target[...]
+        part = place // share_rows
+        seg = slot_of(owner[...], orders[which], ny) * share_rows + place - part * share_rows
+        seg = part * part_rows + seg
 
         def body(i, carry):
             start = pl.multiple_of(i * hot_rows, hot_rows)
@@ -294,18 +300,25 @@
 
         lax.fori_loop(0, seg_total // hot_rows, body, 0)
 
-    def sum_blocks(which, slot, target):
+    def sum_blocks(which, slot, part):
+        goal = chains[part * 3 + slot][1][0]
+
         def body(i, carry):
             start = pl.multiple_of(i * hot_rows, hot_rows)
             both = jnp.dot(
-                hot[which, pl.ds(start, hot_rows), :],
+                hot[which, pl.ds(pl.multiple_of(part * part_rows + start, hot_rows), hot_rows), :],
                 pay[slot],
                 preferred_element_type=jnp.float32,
             )
-            target[pl.ds(start, hot_rows), :] = both[:, :width] + both[:, width:]
+            goal[pl.ds(start, hot_rows), :] = both[:, :width] + both[:, width:]
             return carry
 
-        lax.fori_loop(0, seg_total // hot_rows, body, 0)
+        lax.fori_loop(0, part_rows // hot_rows, body, 0)
+        start_stage(chains[part * 3 + slot], 0)
+
+    def end_stages(slot, stage):
+        for part in range(PARTS):
+            end_stage(chains[part * 3 + slot], stage)
 
     for load in loads[6:9]:
         load.wait()
@@ -313,8 +326,8 @@
     high, low = split_two(pw[...])
     pay[2, :, pl.ds(0, width)] = high
     pay[2, :, pl.ds(width, width)] = low
-    sum_blocks(0, 2, chains[2][1][0])
-    start_stage(chains[2], 0)
+    for part in range(PARTS):
+        sum_blocks(0, 2, part)
     for load in loads[3:6]:
         load.wait()
 
@@ -407,7 +420,7 @@
     halo_start(halo_top2)
 
     build_hot(1)
-    end_stage(chains[2], 0)
+    end_stages(2, 0)
     for load in loads[9:12]:
         load.wait()
     groups = enth.shape[1] // width
@@ -431,16 +444,7 @@
         ratios[layer(k), :] = ratio
         return ratio, value, rate_next, inner
 
-    rate_top = rate_of(0)
-    rate_next = rate_of(1)
-    inner = 0.5 * (rate_top + rate_next)
-    pivot = 1.0 / (1.0 + rate_top + inner)
-    value = (values[layer(0), :] + rate_top * surf[...]) * pivot
-    ratio = -inner * pivot
-    values[layer(0), :] = value
-    ratios[layer(0), :] = ratio
     last = layers - 1
-    state = lax.fori_loop(1, last, eliminate, (ratio, value, rate_next, inner))
 
     halo_wait(halo_top2)
     for q in range(2):
@@ -452,18 +456,18 @@
     for load in loads[12:]:
         load.wait()
 
-    part = 64
+    batch = 64
 
     def pairs(i, carry):
-        at = pl.ds(pl.multiple_of(i * part, part), part)
+        at = pl.ds(pl.multiple_of(i * batch, batch), batch)
         place = pcol[at, :]
         place_row = place // ci
         place_col = place - place_row * ci
         weight = pw[at, :]
         for slot, table in ((0, mean_melt), (1, mean_base)):
-            found = jnp.zeros((part, width), jnp.float32)
+            found = jnp.zeros((batch, width), jnp.float32)
             for r in range(cj):
-                line = jnp.broadcast_to(table[r : r + 1], (part, ci))
+                line = jnp.broadcast_to(table[r : r + 1], (batch, ci))
                 there = jnp.take_along_axis(
                     line, place_col, axis=1, mode="promise_in_bounds"
                 )
@@ -473,18 +477,20 @@
             pay[slot, at, pl.ds(width, width)] = low
         return carry
 
-    lax.fori_loop(0, blocks // part, pairs, 0)
-    for slot in range(2):
-        sum_blocks(slot, slot, chains[slot][1][0])
-        start_stage(chains[slot], 0)
+    lax.fori_loop(0, blocks // batch, pairs, 0)
+    for part in range(PARTS):
+        for slot in range(2):
+            sum_blocks(slot, slot, part)
 
     halo2 = halo(1, row_send2, row_recv2, col_send2, col_recv2)
 
-    def first_spread():
+    def first_couple():
         halo_wait(halo1)
         for q in range(3):
             spread_edge(q, col_recv, edge)
         loop(0, chunks, functools.partial(couple, row_recv, edge))
+
+    def first_spread():
         loop(0, chunks, functools.partial(spread, (temp, salt), row_recv, edge))
 
     def first_mix():
@@ -507,9 +513,24 @@
         saves[0].start()
         saves[1].start()
 
-    ratio_end, value_end, rate_end, inner_end = state
-
-    def back_terms():
+    middle = 1 + (last - 1) // 2
+
+    def forward_first():
+        rate_top = rate_of(0)
+        rate_next = rate_of(1)
+        inner = 0.5 * (rate_top + rate_next)
+        pivot = 1.0 / (1.0 + rate_top + inner)
+        value = (values[layer(0), :] + rate_top * surf[...]) * pivot
+        ratio = -inner * pivot
+        values[layer(0), :] = value
+        ratios[layer(0), :] = ratio
+        return lax.fori_loop(1, middle, eliminate, (ratio, value, rate_next, inner))
+
+    def forward_rest(state):
+        return lax.fori_loop(middle, last, eliminate, state)
+
+    def back_terms(state):
+        ratio_end, value_end, _, _ = state
         ratios[layer(last - 1), :] = -ratio_end
 
         def body(n, carry):
@@ -528,31 +549,42 @@
         ratios[layer(last), :] = jnp.ones((groups, width), jnp.float32)
         return last_side
 
-    side_box = []
-    fill = [
-        first_spread,
-        first_mix,
-        lambda: side_box.append(back_terms()),
-        second_step,
+    stages = len(orders[0])
+
+    def advance(stage):
+        for part in range(PARTS):
+            for slot in range(2):
+                end_stage(chains[part * 3 + slot], stage)
+        if stage + 1 < stages:
+            end_stages(2, stage + 1)
+
+    first_couple()
+    advance(0)
+    first_spread()
+    first_mix()
+    state = forward_first()
+    if stages > 1:
+        advance(1)
+    state = forward_rest(state)
+    if stages > 2:
+        advance(2)
+    last_side = back_terms(state)
+    second_step()
+    for stage in range(3, stages):
+        advance(stage)
+    ratio_end, value_end, _, inner_end = state
+
+    share = 1.0 / area[...]
+    sums = [
+        jnp.concatenate([chains[part * 3 + slot][1][-1][...] for part in range(PARTS)], axis=0)
+        for slot in range(3)
     ]
-    stages = len(orders[0])
-    for stage in range(stages):
-        if stage < len(fill):
-            fill[stage]()
-        end_stage(chains[0], stage)
-        end_stage(chains[1], stage)
-        if stage + 1 < stages:
-            end_stage(chains[2], stage + 1)
-    for work in fill[stages:]:
-        work()
-
-    share = 1.0 / area[...]
-    melt_sum = chains[0][1][-1][...] * share
-    base_sum = chains[1][1][-1][...] * share
-    cover_sum = chains[2][1][-1][...] * share
+    melt_sum = sums[0] * share
+    base_sum = sums[1] * share
+    cover_sum = sums[2] * share
     out_melt[...] = melt_sum
     pivot = 1.0 / (1.0 + inner_end + cover_sum + inner_end * ratio_end)
-    last_layer[...] = (side_box[0] + base_sum + inner_end * value_end) * pivot
+    last_layer[...] = (last_side + base_sum + inner_end * value_end) * pivot
     for g in range(groups):
         rows = pl.ds(g * layers, layers)
         solved = values[rows, :] + ratios[rows, :] * last_layer[pl.ds(g, 1), :]
@@ -571,15 +603,20 @@
 
 
 def store(*refs):
-    count = len(refs) // 2
-    sem = refs[-1]
-    copies = [
-        pltpu.make_async_copy(src, dst, sem.at[i])
-        for i, (src, dst) in enumerate(zip(refs[:count], refs[count:-1]))
-    ]
-    for copy in copies:
+    count = len(refs) // 3
+    sems = refs[3 * count]
+    inward = []
+    outward = []
+    for i in range(count):
+        src, dst, held = refs[i], refs[count + i], refs[2 * count + i]
+        inward.append(pltpu.make_async_copy(src, held, sems.at[0, i]))
+        outward.append(pltpu.make_async_copy(held, dst, sems.at[1, i]))
+    for copy in inward:
         copy.start()
-    for copy in copies:
+    for first, then in zip(inward, outward):
+        first.wait()
+        then.start()
+    for copy in outward:
         copy.wait()
 
 
@@ -665,8 +702,8 @@
         pltpu.VMEM((layers * targets, width), f32),
         pltpu.VMEM((layers * targets, width), f32),
     ]
-    for order in (orders[0], orders[1], orders[0]):
-        rows = live_rows(order, total)
+    for order in (orders[0], orders[1], orders[0]) * PARTS:
+        rows = live_rows(order, total // PARTS)
         scratch += [pltpu.VMEM((n, width), f32) for n in rows]
         scratch += [
             pltpu.VMEM((radix - 1, n, width), f32)
@@ -692,7 +729,8 @@
         out_shape=results,
         in_specs=[hbm] * 4,
         out_specs=(hbm,) * 4,
-        scratch_shapes=[pltpu.SemaphoreType.DMA((4,))],
+        scratch_shapes=[pltpu.VMEM(leaf.shape, leaf.dtype) for leaf in results]
+        + [pltpu.SemaphoreType.DMA((2, 4))],
         compiler_params=pltpu.CompilerParams(vmem_limit_bytes=LIMIT),
     )(*made)
     return (

time: 72.3 us -> 36.2 us (0.50)
  Pallas kernels: 71.5 us -> 35.4 us
    pallas_call x1, Pallas kernels: 37.4 us -> 2.16 us  [local(): pl.pallas_call(store, out_shape=results, in_specs=[hbm] * 4, out_specs=(h...]
    pallas_call x1, Pallas kernels: 34.1 us -> 33.3 us  [local(): pl.pallas_call(functools.partial(kernel, sizes, orders), out_shape=result...]
where the time goes in v3:
time: 36.2 us; the launch traced here: 36.1 us
  Pallas kernels  35.4 us (98%)
  between operations  0.64 us (2%)
    pallas_call x1, Pallas kernels, local(): pl.pallas_call(functools.partial(kernel, sizes, orders), out_shape=result...  33.3 us
    pallas_call x1, Pallas kernels, local(): pl.pallas_call(store, out_shape=results, in_specs=[hbm] * 4, out_specs=(h...  2.16 us

profile of v3, /device:TPU:0, one launch (start us, length us, event | category | flops | bytes accessed | tf_op | source)
XLA Modules:
  0.0 36.1 jit_solution(6240188132818273821)
XLA Ops:
  0.6 33.3 %shard_map.165 = (f32[512,128]{1,0:T(8,128)}, f32[512,128]{1,0:T(8,128)}, f32[40,4096]{1,0:T(8,128)}, f32[32,128]{1,0:T(8,128)}) custom-call(f32[512,128]{1,0:T(8,128)} %bitcast.11, f32[512,128]{1,0:T(8,128)} %bitcast.12, s32[512,128]{1,0:T(8,128)} %bitcast.13, f32[8,128]{1,0:T(8,128)} %refs_3_.1, f32[8,128]{1,0:T(8,128)} %refs_4_.1, f32[8,128]{1,0:T(8,128)} %refs_5_.1, ...), custom_call_target="tpu_custom_call" | custom-call | tf_op jit(solution)/shard_map/pallas_call | solution.py:717
  33.9 2.2 %shard_map.166 = (f32[512,128]{1,0:T(8,128)}, f32[512,128]{1,0:T(8,128)}, f32[40,4096]{1,0:T(8,128)}, f32[32,128]{1,0:T(8,128)}) custom-call(f32[512,128]{1,0:T(8,128)} %get-tuple-element.12.refs_0_, f32[512,128]{1,0:T(8,128)} %get-tuple-element.13.refs_1_, f32[40,4096]{1,0:T(8,128)} %get-tuple-element.14.refs_2_, f32[32,128]{1,0:T(8,128)} %get-tuple-element.15.refs_3_), custom_call_target="tpu_custom_call" | custom-call | tf_op jit(solution)/shard_map/pallas_call | solution.py:727

commit v4 on v3

--- a/solution.py
+++ b/solution.py
@@ -42,6 +42,16 @@
     return (heat_flux, salt_flux, boundary_temp * wet_top)
 
 
+def quotient(value, size):
+    if size & (size - 1):
+        return value // size
+    return lax.shift_right_logical(value, size.bit_length() - 1)
+
+
+def remainder(value, size):
+    return value - quotient(value, size) * size if size & (size - 1) else value & (size - 1)
+
+
 def digits(axis, size):
     found = []
     base = 1
@@ -64,10 +74,10 @@
 
 
 def slot_of(owner, order, ny):
-    coord = {"gx": owner // ny, "gy": owner % ny}
+    coord = {"gx": quotient(owner, ny), "gy": remainder(owner, ny)}
     place = jnp.zeros_like(owner)
     for axis, base, radix in order:
-        place = place * radix + (coord[axis] // base) % radix
+        place = place * radix + remainder(quotient(coord[axis], base), radix)
     return place
 
 
@@ -76,6 +86,12 @@
     for _, _, radix in order:
         rows.append(rows[-1] // radix)
     return rows
+
+
+def inverse(value):
+    guess = pl.reciprocal(value, approx=True)
+    guess = guess * (2.0 - value * guess)
+    return guess * (2.0 - value * guess)
 
 
 def split_two(value):
@@ -233,9 +249,6 @@
 
     halo_top1 = halo(2, row_top, row_top_in, col_top, col_top_in)
     halo_start(halo_top1)
-    pack_all(row_send, col_send)
-    halo1 = halo(0, row_send, row_recv, col_send, col_recv)
-    halo_start(halo1)
 
     def make_copies(chain, stage):
         order, live, got, send_sem, recv_sem = chain
@@ -275,8 +288,8 @@
         if stage + 1 < len(order):
             start_stage(chain, stage + 1)
 
-    def drain(chain):
-        for stage in range(len(chain[0])):
+    def drain(chain, stages_done):
+        for stage in stages_done:
             for copy in make_copies(chain, stage):
                 copy.wait_send()
 
@@ -285,35 +298,55 @@
     share_rows = targets // PARTS
     hot_rows = min(256, part_rows)
 
-    def build_hot(which):
+    def build_hot():
         place = target[...]
-        part = place // share_rows
-        seg = slot_of(owner[...], orders[which], ny) * share_rows + place - part * share_rows
-        seg = part * part_rows + seg
+        seg = slot_of(owner[...], orders[0], ny) * share_rows + remainder(place, share_rows)
+        seg = quotient(place, share_rows) * part_rows + seg
 
         def body(i, carry):
             start = pl.multiple_of(i * hot_rows, hot_rows)
             row = lax.broadcasted_iota(jnp.int32, (hot_rows, blocks), 0) + start
             hit = (row == seg).astype(jnp.float32)
-            hot[which, pl.ds(start, hot_rows), :] = hit.astype(jnp.bfloat16)
+            hot[pl.ds(start, hot_rows), :] = hit.astype(jnp.bfloat16)
             return carry
 
         lax.fori_loop(0, seg_total // hot_rows, body, 0)
 
-    def sum_blocks(which, slot, part):
-        goal = chains[part * 3 + slot][1][0]
-
-        def body(i, carry):
-            start = pl.multiple_of(i * hot_rows, hot_rows)
+    def placed(order):
+        common = 0
+        while common < len(order) and order[-1 - common] == orders[0][-1 - common]:
+            common += 1
+        run = share_rows
+        for _, _, radix in order[len(order) - common :]:
+            run *= radix
+        head = orders[0][: len(order) - common]
+        goals = []
+        for n in range(part_rows // run):
+            left = n
+            at = {}
+            for digit in reversed(head):
+                at[digit] = left % digit[2]
+                left //= digit[2]
+            goal = 0
+            for digit in order[: len(order) - common]:
+                goal = goal * digit[2] + at[digit]
+            goals.append(goal * run)
+        return run, goals
+
+    def sum_blocks(slot, part):
+        order, live = chains[part * 3 + slot][:2]
+        run, goals = placed(order)
+        step = min(run, hot_rows)
+        for start in range(0, part_rows, hot_rows):
             both = jnp.dot(
-                hot[which, pl.ds(pl.multiple_of(part * part_rows + start, hot_rows), hot_rows), :],
+                hot[pl.ds(part * part_rows + start, hot_rows), :],
                 pay[slot],
                 preferred_element_type=jnp.float32,
             )
-            goal[pl.ds(start, hot_rows), :] = both[:, :width] + both[:, width:]
-            return carry
-
-        lax.fori_loop(0, part_rows // hot_rows, body, 0)
+            both = both[:, :width] + both[:, width:]
+            for piece in range(0, hot_rows, step):
+                n, inside = divmod(start + piece, run)
+                live[0][pl.ds(goals[n] + inside, step), :] = both[piece : piece + step]
         start_stage(chains[part * 3 + slot], 0)
 
     def end_stages(slot, stage):
@@ -322,12 +355,12 @@
 
     for load in loads[6:9]:
         load.wait()
-    build_hot(0)
+    build_hot()
     high, low = split_two(pw[...])
     pay[2, :, pl.ds(0, width)] = high
     pay[2, :, pl.ds(width, width)] = low
     for part in range(PARTS):
-        sum_blocks(0, 2, part)
+        sum_blocks(2, part)
     for load in loads[3:6]:
         load.wait()
 
@@ -419,7 +452,9 @@
     halo_top2 = halo(3, row_top2, row_top_in2, col_top2, col_top_in2)
     halo_start(halo_top2)
 
-    build_hot(1)
+    pack_all(row_send, col_send)
+    halo1 = halo(0, row_send, row_recv, col_send, col_recv)
+    halo_start(halo1)
     end_stages(2, 0)
     for load in loads[9:12]:
         load.wait()
@@ -437,7 +472,7 @@
         ratio, value, rate, inner_up = carry
         rate_next = rate_of(k + 1)
         inner = 0.5 * (rate + rate_next)
-        pivot = 1.0 / (1.0 + inner_up + inner + inner_up * ratio)
+        pivot = inverse(1.0 + inner_up + inner + inner_up * ratio)
         value = (values[layer(k), :] + inner_up * value) * pivot
         ratio = -inner * pivot
         values[layer(k), :] = value
@@ -461,8 +496,8 @@
     def pairs(i, carry):
         at = pl.ds(pl.multiple_of(i * batch, batch), batch)
         place = pcol[at, :]
-        place_row = place // ci
-        place_col = place - place_row * ci
+        place_row = quotient(place, ci)
+        place_col = remainder(place, ci)
         weight = pw[at, :]
         for slot, table in ((0, mean_melt), (1, mean_base)):
             found = jnp.zeros((batch, width), jnp.float32)
@@ -480,7 +515,7 @@
     lax.fori_loop(0, blocks // batch, pairs, 0)
     for part in range(PARTS):
         for slot in range(2):
-            sum_blocks(slot, slot, part)
+            sum_blocks(slot, part)
 
     halo2 = halo(1, row_send2, row_recv2, col_send2, col_recv2)
 
@@ -501,19 +536,21 @@
             pack(q, first.at[q], 0, row_send2, col_send2)
         halo_start(halo2)
 
-    def second_step():
+    def second_spread():
         halo_wait(halo2)
         for q in range(2):
             spread_edge(q, col_recv2, edge)
         sources = (first.at[0], first.at[1])
         loop(0, chunks, functools.partial(spread, sources, row_recv2, edge))
+
+    def second_mix():
         loop(0, chunks, lambda c: mix(c, (out_temp, out_salt)))
         out_temp[pl.ds(0, cj), :] = new_top_temp
         out_salt[pl.ds(0, cj), :] = new_top_salt
         saves[0].start()
         saves[1].start()
 
-    middle = 1 + (last - 1) // 2
+    middle = 1 + (last - 1) // 4 * 2
 
     def forward_first():
         rate_top = rate_of(0)
@@ -524,10 +561,10 @@
         ratio = -inner * pivot
         values[layer(0), :] = value
         ratios[layer(0), :] = ratio
-        return lax.fori_loop(1, middle, eliminate, (ratio, value, rate_next, inner))
+        return lax.fori_loop(1, middle, eliminate, (ratio, value, rate_next, inner), unroll=2)
 
     def forward_rest(state):
-        return lax.fori_loop(middle, last, eliminate, state)
+        return lax.fori_loop(middle, last, eliminate, state, unroll=2)
 
     def back_terms(state):
         ratio_end, value_end, _, _ = state
@@ -543,7 +580,7 @@
             ratios[layer(k), :] = slope
             return level, slope
 
-        lax.fori_loop(0, last - 1, body, (value_end, -ratio_end))
+        lax.fori_loop(0, last - 1, body, (value_end, -ratio_end), unroll=2)
         last_side = values[layer(last), :]
         values[layer(last), :] = jnp.zeros((groups, width), jnp.float32)
         ratios[layer(last), :] = jnp.ones((groups, width), jnp.float32)
@@ -551,25 +588,30 @@
 
     stages = len(orders[0])
 
-    def advance(stage):
+    def advance(stage, between=None):
+        made = None
         for part in range(PARTS):
             for slot in range(2):
                 end_stage(chains[part * 3 + slot], stage)
+            if part == 0 and between is not None:
+                made = between()
         if stage + 1 < stages:
             end_stages(2, stage + 1)
+        return made
 
     first_couple()
     advance(0)
     first_spread()
     first_mix()
-    state = forward_first()
-    if stages > 1:
-        advance(1)
+    state = advance(1, forward_first) if stages > 1 else forward_first()
     state = forward_rest(state)
     if stages > 2:
         advance(2)
     last_side = back_terms(state)
-    second_step()
+    second_spread()
+    second_mix()
+    for chain in chains:
+        drain(chain, range(min(2, stages)))
     for stage in range(3, stages):
         advance(stage)
     ratio_end, value_end, _, inner_end = state
@@ -597,7 +639,7 @@
     halo_done(halo1)
     halo_done(halo2)
     for chain in chains:
-        drain(chain)
+        drain(chain, range(min(2, stages), stages))
     for save in saves:
         save.wait()
 
@@ -697,7 +739,7 @@
         pltpu.VMEM((2, 2, CHUNK, ci), f32),
         pltpu.VMEM((2, 8, top_cells), f32),
         pltpu.VMEM((2, 8, top_cells), f32),
-        pltpu.VMEM((2, total, blocks), jnp.bfloat16),
+        pltpu.VMEM((total, blocks), jnp.bfloat16),
         pltpu.VMEM((3, blocks, 2 * width), jnp.bfloat16),
         pltpu.VMEM((layers * targets, width), f32),
         pltpu.VMEM((layers * targets, width), f32),

time: 36.2 us -> 35.5 us (0.981)
  Pallas kernels: 35.4 us -> 34.7 us
    pallas_call x1, Pallas kernels: 33.3 us -> 32.6 us  [local(): pl.pallas_call(functools.partial(kernel, sizes, orders), out_shape=result...]
where the time goes in v4:
time: 35.5 us; the launch traced here: 35.4 us
  Pallas kernels  34.7 us (98%)
  between operations  0.64 us (2%)
    pallas_call x1, Pallas kernels, local(): pl.pallas_call(functools.partial(kernel, sizes, orders), out_shape=result...  32.6 us
    pallas_call x1, Pallas kernels, local(): pl.pallas_call(store, out_shape=results, in_specs=[hbm] * 4, out_specs=(h...  2.16 us

profile of v4, /device:TPU:0, one launch (start us, length us, event | category | flops | bytes accessed | tf_op | source)
XLA Modules:
  0.0 35.4 jit_solution(9936602736198115288)
XLA Ops:
  0.6 32.6 %shard_map.165 = (f32[512,128]{1,0:T(8,128)}, f32[512,128]{1,0:T(8,128)}, f32[40,4096]{1,0:T(8,128)}, f32[32,128]{1,0:T(8,128)}) custom-call(f32[512,128]{1,0:T(8,128)} %bitcast.11, f32[512,128]{1,0:T(8,128)} %bitcast.12, s32[512,128]{1,0:T(8,128)} %bitcast.13, f32[8,128]{1,0:T(8,128)} %refs_3_.1, f32[8,128]{1,0:T(8,128)} %refs_4_.1, f32[8,128]{1,0:T(8,128)} %refs_5_.1, ...), custom_call_target="tpu_custom_call" | custom-call | tf_op jit(solution)/shard_map/pallas_call | solution.py:759
  33.2 2.2 %shard_map.166 = (f32[512,128]{1,0:T(8,128)}, f32[512,128]{1,0:T(8,128)}, f32[40,4096]{1,0:T(8,128)}, f32[32,128]{1,0:T(8,128)}) custom-call(f32[512,128]{1,0:T(8,128)} %get-tuple-element.12.refs_0_, f32[512,128]{1,0:T(8,128)} %get-tuple-element.13.refs_1_, f32[40,4096]{1,0:T(8,128)} %get-tuple-element.14.refs_2_, f32[32,128]{1,0:T(8,128)} %get-tuple-element.15.refs_3_), custom_call_target="tpu_custom_call" | custom-call | tf_op jit(solution)/shard_map/pallas_call | solution.py:769

commit v5 on v4

--- a/solution.py
+++ b/solution.py
@@ -70,7 +70,8 @@
     gx = digits("gx", nx)
     first = gy + gx
     second = gy[:1] + gx[:1] + gy[1:] + gx[1:]
-    return (first, second)
+    third = gy[:1] + gx[-1:] + gy[1:] + gx[:-1]
+    return (first, second, third)
 
 
 def slot_of(owner, order, ny):
@@ -133,7 +134,7 @@
     (row_top2, row_top_in2, col_top2, col_top_in2) = take(4)
     (hot, pay, ratios, values) = take(4)
     chains = []
-    for order in (orders[0], orders[1], orders[0]) * PARTS:
+    for order in orders * PARTS:
         live = take(len(order) + 1)
         got = take(len(order))
         send_sem, recv_sem = take(2)
@@ -595,8 +596,8 @@
                 end_stage(chains[part * 3 + slot], stage)
             if part == 0 and between is not None:
                 made = between()
-        if stage + 1 < stages:
-            end_stages(2, stage + 1)
+        if stage > 0:
+            end_stages(2, stage)
         return made
 
     first_couple()
@@ -744,7 +745,7 @@
         pltpu.VMEM((layers * targets, width), f32),
         pltpu.VMEM((layers * targets, width), f32),
     ]
-    for order in (orders[0], orders[1], orders[0]) * PARTS:
+    for order in orders * PARTS:
         rows = live_rows(order, total // PARTS)
         scratch += [pltpu.VMEM((n, width), f32) for n in rows]
         scratch += [

time: 35.5 us -> 35.3 us (level)
  no operation moved by 1% of the time
where the time goes in v5:
time: 35.3 us; the launch traced here: 35.1 us
  Pallas kernels  34.5 us (98%)
  between operations  0.64 us (2%)
    pallas_call x1, Pallas kernels, local(): pl.pallas_call(functools.partial(kernel, sizes, orders), out_shape=result...  32.3 us
    pallas_call x1, Pallas kernels, local(): pl.pallas_call(store, out_shape=results, in_specs=[hbm] * 4, out_specs=(h...  2.16 us

profile of v5, /device:TPU:0, one launch (start us, length us, event | category | flops | bytes accessed | tf_op | source)
XLA Modules:
  0.0 35.1 jit_solution(14024067978907980392)
XLA Ops:
  0.6 32.3 %shard_map.165 = (f32[512,128]{1,0:T(8,128)}, f32[512,128]{1,0:T(8,128)}, f32[40,4096]{1,0:T(8,128)}, f32[32,128]{1,0:T(8,128)}) custom-call(f32[512,128]{1,0:T(8,128)} %bitcast.11, f32[512,128]{1,0:T(8,128)} %bitcast.12, s32[512,128]{1,0:T(8,128)} %bitcast.13, f32[8,128]{1,0:T(8,128)} %refs_3_.1, f32[8,128]{1,0:T(8,128)} %refs_4_.1, f32[8,128]{1,0:T(8,128)} %refs_5_.1, ...), custom_call_target="tpu_custom_call" | custom-call | tf_op jit(solution)/shard_map/pallas_call | solution.py:760
  32.9 2.2 %shard_map.166 = (f32[512,128]{1,0:T(8,128)}, f32[512,128]{1,0:T(8,128)}, f32[40,4096]{1,0:T(8,128)}, f32[32,128]{1,0:T(8,128)}) custom-call(f32[512,128]{1,0:T(8,128)} %get-tuple-element.12.refs_0_, f32[512,128]{1,0:T(8,128)} %get-tuple-element.13.refs_1_, f32[40,4096]{1,0:T(8,128)} %get-tuple-element.14.refs_2_, f32[32,128]{1,0:T(8,128)} %get-tuple-element.15.refs_3_), custom_call_target="tpu_custom_call" | custom-call | tf_op jit(solution)/shard_map/pallas_call | solution.py:770
